TPU v7x, 256 devices: a whole 4x4x8 slice. The times are simulated.
256 devices in a mesh: dp: 4 (over y), bal: 64 (over z, x, core).
Axes of the slice: x: 4, y: 4, z: 8, core: 2. Of those that a mesh axis runs over, the one named last changes fastest.
Arguments:
- queries: bfloat16 [131072, 1024], P(('dp', 'bal')), may hold values from -6 to 6
- keys: bfloat16 [131072, 1024], P(('dp', 'bal')), may hold values from -6 to 6
- values: bfloat16 [131072, 1024], P(('dp', 'bal')), may hold values from -6 to 6
- gates: bfloat16 [131072, 1024], P(('dp', 'bal')), may hold values from -24 to 24
- cotangent: bfloat16 [131072, 1024], P(('dp', 'bal')), may hold values from -6 to 6
- hist_len: int32 [256, 8], P(('dp', 'bal')), may hold values from 1 to 256, 512 in all within a row
- token_owner: int32 [131072], P(('dp', 'bal')), may hold values from 0 to 63, as said below
- token_row: int32 [131072], P(('dp', 'bal')), may hold values from 0 to 511
- w_out: bfloat16 [1024, 1024], P('dp'), may hold values from -0.1875 to 0.1875
Outputs:
- output: bfloat16 [131072, 1024], P(('dp', 'bal'))
- grad_queries: bfloat16 [131072, 1024], P(('dp', 'bal'))
- grad_keys: bfloat16 [131072, 1024], P(('dp', 'bal'))
- grad_values: bfloat16 [131072, 1024], P(('dp', 'bal'))
- grad_gates: bfloat16 [131072, 1024], P(('dp', 'bal'))
- grad_weight: float32 [1024, 1024], P('dp')
Inputs may be any that keep to these rules, and one draw needn't show every extreme that they name: Within each user group, every owner receives exactly 512 tokens, and the pairs (token_owner, token_row) are all different. The 512 tokens of one source device hold at most 16 tokens for one owner, and every source device holds exactly 16 for some owner.
All inputs are finite; a program needn't handle non-finite values.
Results may differ from a plain program's by a relative error of at most 0.014.
Values may be sent and summed in bfloat16 or wider, within the bound.
A program may use at most 128 MiB of HBM per device.

v0:
```python
import math

import jax
import jax.numpy as jnp
from jax import lax
from jax.sharding import PartitionSpec as P

HEAD = 128


EPSILON = 1e-05


def history_mask(lengths, row_count):
    history_end = jnp.cumsum(lengths)
    positions = jnp.arange(row_count, dtype=jnp.int32)
    history_id = jnp.sum((positions[:, None] >= history_end[None, :]).astype(jnp.int32), axis=1)
    return (history_id[:, None] == history_id[None, :]) & (positions[:, None] >= positions[None, :])


def split_heads(tensor):
    return tensor.reshape(tensor.shape[0], -1, HEAD)


def scores_of(own_q, own_k):
    return jnp.einsum(
        "ihe,jhe->hij", split_heads(own_q), split_heads(own_k), preferred_element_type=jnp.float32
    ) / math.sqrt(HEAD)


def owner_forward(own_q, own_k, own_v, allowed):
    scores = scores_of(own_q, own_k)
    weights = jnp.where(allowed[None], jax.nn.silu(scores), 0.0).astype(jnp.bfloat16)
    attended = jnp.einsum(
        "hij,jhe->ihe", weights, split_heads(own_v), preferred_element_type=jnp.float32
    )
    return attended.reshape(own_q.shape[0], -1).astype(jnp.bfloat16)


def owner_backward(own_q, own_k, own_v, allowed, grad_own):
    row_count = own_q.shape[0]
    scores = scores_of(own_q, own_k)
    sigmoid_val = jax.nn.sigmoid(scores)
    weights = jnp.where(allowed[None], jax.nn.silu(scores), 0.0).astype(jnp.bfloat16)
    grad_heads = split_heads(grad_own)
    grad_probs = jnp.einsum(
        "ihe,jhe->hij", grad_heads, split_heads(own_v), preferred_element_type=jnp.float32
    )
    grad_scores = jnp.where(
        allowed[None], grad_probs * sigmoid_val * (1.0 + scores * (1.0 - sigmoid_val)), 0.0
    ) / math.sqrt(HEAD)
    grad_scores = grad_scores.astype(jnp.bfloat16)
    grad_v = jnp.einsum("hij,ihe->jhe", weights, grad_heads, preferred_element_type=jnp.float32)
    grad_q = jnp.einsum(
        "hij,jhe->ihe", grad_scores, split_heads(own_k), preferred_element_type=jnp.float32
    )
    grad_k = jnp.einsum(
        "hij,ihe->jhe", grad_scores, split_heads(own_q), preferred_element_type=jnp.float32
    )
    return (
        grad_q.reshape(row_count, -1).astype(jnp.bfloat16),
        grad_k.reshape(row_count, -1).astype(jnp.bfloat16),
        grad_v.reshape(row_count, -1).astype(jnp.bfloat16),
    )


def normalize(attended):
    wide = attended.astype(jnp.float32)
    centered = wide - jnp.mean(wide, axis=-1, keepdims=True)
    inverse = lax.rsqrt(jnp.mean(centered * centered, axis=-1, keepdims=True) + EPSILON)
    return (centered * inverse, inverse)


def gating_backward(grad_hidden, normed, inverse, gates):
    grad_gates = (grad_hidden * normed).astype(jnp.bfloat16)
    grad_normed = grad_hidden * gates.astype(jnp.float32)
    mean_grad = jnp.mean(grad_normed, axis=-1, keepdims=True)
    mean_cross = jnp.mean(grad_normed * normed, axis=-1, keepdims=True)
    grad_attended = (grad_normed - mean_grad - normed * mean_cross) * inverse
    return (grad_gates, grad_attended.astype(jnp.bfloat16))


def project(gated, cotangent, w_out):
    full_weight = lax.all_gather(w_out, "dp", axis=0, tiled=True)
    output = jnp.dot(gated, full_weight, preferred_element_type=jnp.float32)
    grad_hidden = lax.dot_general(
        cotangent, full_weight, (((1,), (1,)), ((), ())), preferred_element_type=jnp.float32
    )
    return (output.astype(jnp.bfloat16), grad_hidden)


def weight_grads(gated, cotangent):
    group_share = lax.psum_scatter(
        lax.dot_general(
            gated, cotangent, (((0,), (0,)), ((), ())), preferred_element_type=jnp.float32
        ).astype(jnp.bfloat16),
        "dp",
        scatter_dimension=0,
        tiled=True,
    ).astype(jnp.float32)
    return lax.psum(group_share, "bal")


def body(queries, keys, values, gates, cotangent, hist_len, token_owner, token_row, w_out):
    row_count = queries.shape[0]
    owner_count = lax.axis_size("bal")
    slot_count = 2 * (row_count // owner_count)
    allowed = history_mask(hist_len[0], row_count)
    matches = (token_owner[:, None] == jnp.arange(owner_count, dtype=jnp.int32)[None, :]).astype(
        jnp.int32
    )
    earlier = jnp.cumsum(matches, axis=0) - matches
    slot_index = token_owner * slot_count + jnp.sum(earlier * matches, axis=1)

    def pack(tensor, filler):
        empty = jnp.full((owner_count * slot_count,) + tensor.shape[1:], filler, tensor.dtype)
        return (
            empty.at[slot_index].set(tensor).reshape((owner_count, slot_count) + tensor.shape[1:])
        )

    def unpack_owner(received, landing):
        flat = received.reshape((owner_count * slot_count,) + received.shape[2:])
        return (
            jnp.zeros((row_count,) + flat.shape[1:], flat.dtype).at[landing].set(flat, mode="drop")
        )

    def to_slots(tensor, landing):
        return jnp.take(tensor, jnp.minimum(landing, row_count - 1), axis=0).reshape(
            owner_count, slot_count, -1
        )

    def from_slots(received):
        return jnp.take(received.reshape(owner_count * slot_count, -1), slot_index, axis=0)

    received = (
        lax.all_to_all(pack(queries, 0), "bal", split_axis=0, concat_axis=0, tiled=True),
        lax.all_to_all(pack(keys, 0), "bal", split_axis=0, concat_axis=0, tiled=True),
        lax.all_to_all(pack(values, 0), "bal", split_axis=0, concat_axis=0, tiled=True),
        lax.all_to_all(pack(token_row, row_count), "bal", split_axis=0, concat_axis=0, tiled=True),
    )
    landing = received[3].reshape(-1)
    own_q, own_k, own_v = [unpack_owner(member, landing) for member in received[:3]]
    attended_own = owner_forward(own_q, own_k, own_v, allowed)
    attended = from_slots(
        lax.all_to_all(
            to_slots(attended_own, landing), "bal", split_axis=0, concat_axis=0, tiled=True
        )
    )
    normed, inverse = normalize(attended)
    gated = (normed * gates.astype(jnp.float32)).astype(jnp.bfloat16)
    output, grad_hidden = project(gated, cotangent, w_out)
    grad_weight = weight_grads(gated, cotangent)
    grad_gates, grad_attended = gating_backward(grad_hidden, normed, inverse, gates)
    grad_own = unpack_owner(
        lax.all_to_all(pack(grad_attended, 0), "bal", split_axis=0, concat_axis=0, tiled=True),
        landing,
    )
    grad_q, grad_k, grad_v = owner_backward(own_q, own_k, own_v, allowed, grad_own)
    returned = (
        lax.all_to_all(to_slots(grad_q, landing), "bal", split_axis=0, concat_axis=0, tiled=True),
        lax.all_to_all(to_slots(grad_k, landing), "bal", split_axis=0, concat_axis=0, tiled=True),
        lax.all_to_all(to_slots(grad_v, landing), "bal", split_axis=0, concat_axis=0, tiled=True),
    )
    return (
        output,
        from_slots(returned[0]),
        from_slots(returned[1]),
        from_slots(returned[2]),
        grad_gates,
        grad_weight,
    )


def solution(mesh):
    return jax.shard_map(
        body,
        mesh=mesh,
        in_specs=(
            P(("dp", "bal"), None),
            P(("dp", "bal"), None),
            P(("dp", "bal"), None),
            P(("dp", "bal"), None),
            P(("dp", "bal"), None),
            P(("dp", "bal"), None),
            P(("dp", "bal")),
            P(("dp", "bal")),
            P("dp", None),
        ),
        out_specs=(
            P(("dp", "bal"), None),
            P(("dp", "bal"), None),
            P(("dp", "bal"), None),
            P(("dp", "bal"), None),
            P(("dp", "bal"), None),
            P("dp", None),
        ),
        check_vma=False,
    )
```

profile of v0, /device:TPU:1, one launch (start us, length us, event | category | flops | bytes accessed | tf_op | source)
XLA Modules:
  0.0 842.7 jit_solution(9189934396201363818)
XLA Ops:
  10.9 2.6 scatter_custom_fusion
  14.2 13.0 %all-to-all-start = ((s32[64,1,16]{2,1,0:T(1,128)}), s32[64,1,16]{2,1,0:T(1,128)S(1)}, u32[]{:S(2)}, u32[]{:S(2)}) async-start(s32[64,1,16]{2,1,0:T(1,128)} %bitcast.2), calls=%async_computation | async-start | bytes 65536 | tf_op jit(solution)/shard_map/all_to_all | solution.py:139
  27.2 4.8 scatter_custom_fusion.1
  32.1 4.5 all-to-all-done
  36.5 5.8 all-to-all-start.1
  42.4 4.8 scatter_custom_fusion.3
  47.2 44.9 %all-to-all-done.1 = bf16[64,16,1024]{2,1,0:T(8,128)(2,1)S(1)} async-done(((bf16[64,16,1024]{2,1,0:T(8,128)(2,1)}), bf16[64,16,1024]{2,1,0:T(8,128)(2,1)S(1)}, u32[]{:S(2)}, u32[]{:S(2)}) %all-to-all-start.1) | async-done | bytes 2097184 | tf_op jit(solution)/shard_map/all_to_all | solution.py:138
  93.3 7.6 all-to-all-start.2
  101.0 4.8 scatter_custom_fusion.5
  105.8 44.5 %all-to-all-done.2 = bf16[64,16,1024]{2,1,0:T(8,128)(2,1)} async-done(((bf16[64,16,1024]{2,1,0:T(8,128)(2,1)}), bf16[64,16,1024]{2,1,0:T(8,128)(2,1)}, u32[]{:S(2)}, u32[]{:S(2)}) %all-to-all-start.2) | async-done | bytes 2097184 | tf_op jit(solution)/shard_map/all_to_all | solution.py:136
  150.3 7.4 all-to-all-start.3
  159.7 6.2 scatter_custom_fusion.2
  165.9 1.3 copy.52
  167.2 6.6 scatter_custom_fusion.4
  174.4 32.9 %all-to-all-done.3 = bf16[64,16,1024]{2,1,0:T(8,128)(2,1)} async-done(((bf16[64,16,1024]{2,1,0:T(8,128)(2,1)}), bf16[64,16,1024]{2,1,0:T(8,128)(2,1)}, u32[]{:S(2)}, u32[]{:S(2)}) %all-to-all-start.3) | async-done | bytes 2097184 | tf_op jit(solution)/shard_map/all_to_all | solution.py:137
  207.3 6.2 scatter_custom_fusion.6
  214.8 6.8 select_convert_fusion
  221.6 1.5 convolution_convert_fusion.5
  224.1 5.4 gather_fusion
  229.4 3.2 broadcast_select_fusion.3
  232.6 7.0 all-to-all-start.4
  240.4 48.9 %all-to-all-done.4 = bf16[64,16,1024]{2,1,0:T(8,128)(2,1)S(1)} async-done(((bf16[64,16,1024]{2,1,0:T(8,128)(2,1)}), bf16[64,16,1024]{2,1,0:T(8,128)(2,1)S(1)}, u32[]{:S(2)}, u32[]{:S(2)}) %all-to-all-start.4) | async-done | bytes 2097184 | tf_op jit(solution)/shard_map/all_to_all | solution.py:145
  289.3 2.8 gather_fusion.1
  292.1 1.7 convert_reduce_fusion
  293.8 1.7 fusion.10
  295.6 4.9 fusion.26
  300.5 5.8 scatter_custom_fusion.7
  306.3 56.8 %all_to_all.49 = bf16[64,16,1024]{2,1,0:T(8,128)(2,1)} all-to-all(bf16[64,16,1024]{2,1,0:T(8,128)(2,1)} %bitcast.78), channel_id=1, replica_groups=mesh['dp'=4,'bal'=64] {'bal'}, dimensions={0} | all-to-all | bytes 4194304 | tf_op jit(solution)/shard_map/all_to_all | solution.py:155
  363.1 6.4 scatter_custom_fusion.8
  370.8 3.4 convolution_convert_fusion.1
  374.2 6.8 multiply_convert_fusion
  381.1 2.4 convolution_convert_fusion.3
  383.5 1.7 convolution_convert_fusion.2
  385.8 5.4 gather_fusion.6
  391.7 5.4 gather_fusion.2
  397.6 5.4 gather_fusion.4
  403.0 4.6 broadcast_select_fusion
  407.6 56.5 %all_to_all.50 = bf16[64,16,1024]{2,1,0:T(8,128)(2,1)S(1)} all-to-all(bf16[64,16,1024]{2,1,0:T(8,128)(2,1)S(1)} %bitcast.76), channel_id=1, replica_groups=mesh['dp'=4,'bal'=64] {'bal'}, dimensions={0} | all-to-all | bytes 4194304 | tf_op jit(solution)/shard_map/all_to_all | solution.py:162
  464.1 7.2 all-to-all-start.6
  471.4 4.5 convolution_convert_fusion
  475.9 45.0 %all-to-all-done.6 = bf16[64,16,1024]{2,1,0:T(8,128)(2,1)} async-done(((bf16[64,16,1024]{2,1,0:T(8,128)(2,1)}), bf16[64,16,1024]{2,1,0:T(8,128)(2,1)}, u32[]{:S(2)}, u32[]{:S(2)}) %all-to-all-start.6) | async-done | bytes 2097184 | tf_op jit(solution)/shard_map/all_to_all | solution.py:160
  520.9 7.6 all-to-all-start.7
  528.6 4.6 convolution_convert_fusion.4
  533.1 286.3 %all-reduce.1 = f32[256,1024]{1,0:T(8,128)} all-reduce(bf16[256,1024]{1,0:T(8,128)(2,1)} %reduce-scatter.2.cloned.1.call-done), channel_id=1, replica_groups=mesh['dp'=4,'bal'=64] {'bal'}, use_global_device_ids=true, to_apply=%region_19.22 | all-reduce | flops 262144 | bytes 1572864 | tf_op jit(solution)/shard_map/psum | solution.py:101
  819.4 2.8 gather_fusion.7
  822.2 4.6 gather_fusion.3
  826.8 5.4 gather_fusion.5
  832.2 3.2 broadcast_select_fusion.4
  (66 shorter events, 14.4 us)
Async XLA Ops:
  7.2 288.5 %copy-start = (bf16[512,1024]{1,0:T(8,128)(2,1)S(1)}, bf16[512,1024]{1,0:T(8,128)(2,1)}, u32[]{:S(2)}) copy-start(bf16[512,1024]{1,0:T(8,128)(2,1)} %param.17) | copy-start | bytes 3145732
  14.2 22.3 %all-to-all-start = ((s32[64,1,16]{2,1,0:T(1,128)}), s32[64,1,16]{2,1,0:T(1,128)S(1)}, u32[]{:S(2)}, u32[]{:S(2)}) async-start(s32[64,1,16]{2,1,0:T(1,128)} %bitcast.2), calls=%async_computation | async-start | bytes 65536 | tf_op jit(solution)/shard_map/all_to_all | solution.py:139
  36.5 55.5 %all-to-all-start.1 = ((bf16[64,16,1024]{2,1,0:T(8,128)(2,1)}), bf16[64,16,1024]{2,1,0:T(8,128)(2,1)S(1)}, u32[]{:S(2)}, u32[]{:S(2)}) async-start(bf16[64,16,1024]{2,1,0:T(8,128)(2,1)} %bitcast.4), calls=%async_computation.1 | async-start | bytes 4194304 | tf_op jit(solution)/shard_map/all_to_all | solution.py:138
  92.0 1.3 copy-start.12
  93.3 57.0 %all-to-all-start.2 = ((bf16[64,16,1024]{2,1,0:T(8,128)(2,1)}), bf16[64,16,1024]{2,1,0:T(8,128)(2,1)}, u32[]{:S(2)}, u32[]{:S(2)}) async-start(bf16[64,16,1024]{2,1,0:T(8,128)(2,1)} %bitcast.9), calls=%async_computation.2 | async-start | bytes 4194304 | tf_op jit(solution)/shard_map/all_to_all | solution.py:136
  150.3 7.4 copy-start.14
  150.3 57.0 %all-to-all-start.3 = ((bf16[64,16,1024]{2,1,0:T(8,128)(2,1)}), bf16[64,16,1024]{2,1,0:T(8,128)(2,1)}, u32[]{:S(2)}, u32[]{:S(2)}) async-start(bf16[64,16,1024]{2,1,0:T(8,128)(2,1)} %bitcast.11), calls=%async_computation.3 | async-start | bytes 4194304 | tf_op jit(solution)/shard_map/all_to_all | solution.py:137
  174.3 47.2 %copy-start.4 = (bf16[512,1024]{0,1:T(8,128)(2,1)}, bf16[512,1024]{0,1:T(8,128)(2,1)S(1)}, u32[]{:S(2)}) copy-start(bf16[512,1024]{0,1:T(8,128)(2,1)S(1)} %copy.65) | copy-start | bytes 3145732
  214.8 6.8 copy-start.6
  221.6 2.0 copy-start.1
  232.6 56.7 %all-to-all-start.4 = ((bf16[64,16,1024]{2,1,0:T(8,128)(2,1)}), bf16[64,16,1024]{2,1,0:T(8,128)(2,1)S(1)}, u32[]{:S(2)}, u32[]{:S(2)}) async-start(bf16[64,16,1024]{2,1,0:T(8,128)(2,1)} %bitcast.77), calls=%async_computation.4 | async-start | bytes 4194304 | tf_op jit(solution)/shard_map/all_to_all | solution.py:145
  239.7 56.0 %all-gather.2.cloned.1.call-start = ((), (), s32[]{:S(2)}) async-start(), calls=%async_computation.10 | async-start | bytes 2621440 | tf_op jit(solution)/shard_map/all_gather | solution.py:84
  292.1 3.5 copy-start.2
  292.1 3.5 copy-start.13
  370.8 3.4 copy-start.7
  370.8 3.4 copy-start.11
  374.2 6.9 copy-start.8
  381.0 2.5 copy-start.5
  385.7 5.4 copy-start.10
  391.7 5.4 copy-start.9
  464.1 56.8 %all-to-all-start.6 = ((bf16[64,16,1024]{2,1,0:T(8,128)(2,1)}), bf16[64,16,1024]{2,1,0:T(8,128)(2,1)}, u32[]{:S(2)}, u32[]{:S(2)}) async-start(bf16[64,16,1024]{2,1,0:T(8,128)(2,1)} %bitcast.75), calls=%async_computation.6 | async-start | bytes 4194304 | tf_op jit(solution)/shard_map/all_to_all | solution.py:160
  471.3 61.8 %reduce-scatter.2.cloned.1.call-start = ((), (), s32[]{:S(2)}) async-start(), calls=%async_computation.11 | async-start | bytes 2621440 | tf_op jit(solution)/shard_map/reduce_scatter | solution.py:93
  520.9 305.9 %all-to-all-start.7 = ((bf16[64,16,1024]{2,1,0:T(8,128)(2,1)}), bf16[64,16,1024]{2,1,0:T(8,128)(2,1)}, u32[]{:S(2)}, u32[]{:S(2)}) async-start(bf16[64,16,1024]{2,1,0:T(8,128)(2,1)} %bitcast.74), calls=%async_computation.7 | async-start | bytes 4194304 | tf_op jit(solution)/shard_map/all_to_all | solution.py:161
  826.8 5.4 copy-start.3
Sparse Core Ops, SparseCore 0:
  242.3 34.5 all-gather.1
  476.0 33.3 reduce-scatter.1
where the time goes:
time: 856 us; the launch traced here: 843 us
  blocking collectives  400 us (47%)
  waiting for transfers between devices  221 us (26%)
  local copies, waits for them, and re-layouts  89.4 us (10%)
  starting transfers between devices  55.9 us (7%)
  matrix products  36.5 us (4%)
  other arithmetic  25.1 us (3%)
  between operations  14.9 us (2%)
    psum x1, blocking collectives, weight_grads(): return lax.psum(group_share, 'bal')  286 us
    all_to_all x1, blocking collectives, body(): lax.all_to_all(pack(grad_attended, 0), 'bal', split_axis=0, concat_axis=0...  56.8 us
    all_to_all x1, blocking collectives, body(): lax.all_to_all(to_slots(grad_v, landing), 'bal', split_axis=0, concat_axi...  56.5 us
    all_to_all x1, waiting for transfers between devices, body(): lax.all_to_all(to_slots(attended_own, landing), 'bal', split_axis=0, conc...  48.9 us
    all_to_all x1, waiting for transfers between devices, body(): lax.all_to_all(to_slots(grad_q, landing), 'bal', split_axis=0, concat_axi...  45 us
    all_to_all x1, waiting for transfers between devices, body(): lax.all_to_all(pack(values, 0), 'bal', split_axis=0, concat_axis=0, tiled...  44.9 us
    all_to_all x1, waiting for transfers between devices, body(): lax.all_to_all(pack(queries, 0), 'bal', split_axis=0, concat_axis=0, tile...  44.5 us
    all_to_all x1, waiting for transfers between devices, body(): lax.all_to_all(pack(keys, 0), 'bal', split_axis=0, concat_axis=0, tiled=T...  32.9 us
  transfers between devices with their start and end apart: 9, of which 6 were waited for; matrix products, arithmetic and copies ran while one was open for 6% of the time, Pallas kernels for 0%

commit v1 on v0

v1 whole, which is shorter than its diff:
```python
import functools
import math

import jax
import jax.numpy as jnp
from jax import lax
from jax.experimental import pallas as pl
from jax.experimental.pallas import tpu as pltpu
from jax.sharding import PartitionSpec as P

HEAD = 128
EPSILON = 1e-05
SLOTS = 16
MESH = pl.DeviceIdType.MESH
F32 = jnp.float32
BF16 = jnp.bfloat16
META = 768


def nn(a, b):
    return lax.dot_general(a, b, (((1,), (0,)), ((), ())), preferred_element_type=F32)


def nt(a, b):
    return lax.dot_general(a, b, (((1,), (1,)), ((), ())), preferred_element_type=F32)


def tn(a, b):
    return lax.dot_general(a, b, (((0,), (0,)), ((), ())), preferred_element_type=F32)


def block_wait(ref, sem):
    pltpu.make_async_copy(ref, ref, sem).wait()


def kernel(
    nz, npeer, ny,
    q_ref, k_ref, v_ref, gates_ref, cot_ref, meta_ref, w_ref,
    out_ref, gq_ref, gk_ref, gv_ref, gg_ref, gw_ref, xback,
    onehot_src, onehot_own, zbuf, xsend, xrecv, own, att_own, wfull, att_full,
    metaz, tsend, trecv, stat_s, stat_r, stat_f,
    dw_send, dw_recv, r1_send, r1_recv, r2_send, r2_recv, gz, gp,
    loc, zin_s, zin_r, xin_s, xin_r, xo_s, xo_r, zo_s, zo_r,
    m_s, m_r, t_s, t_r, w_s, w_r, sa_s, sa_r, sb_s, sb_r,
    dy_s, dy_r, dp_s, dp_r, dz_s, dz_r, az_s, az_r, ap_s, ap_r,
):
    y = lax.axis_index("dp")
    b = lax.axis_index("bal")
    z = b // npeer
    p = lax.rem(b, npeer)
    rows = q_ref.shape[0]
    slots = npeer * nz * SLOTS
    scale = 1.0 / math.sqrt(HEAD)

    def zpeer(d):
        return lax.rem(z + d, nz)

    def ppeer(d):
        return lax.rem(p + d, npeer)

    def ypeer(d):
        return lax.rem(y + d, ny)

    def zdev(at):
        return (y, at * npeer + p)

    def pdev(at):
        return (y, z * npeer + at)

    def ydev(at):
        return (at, b)

    def columns(at):
        return pl.ds(pl.multiple_of(at * HEAD, HEAD), HEAD)

    def remote(src, dst, ssem, rsem, device):
        copy = pltpu.make_async_remote_copy(
            src_ref=src, dst_ref=dst, send_sem=ssem, recv_sem=rsem,
            device_id=device, device_id_type=MESH,
        )
        copy.start()
        return copy

    barrier = pltpu.get_barrier_semaphore()
    for d in range(1, nz):
        pl.semaphore_signal(barrier, inc=1, device_id=zdev(zpeer(d)), device_id_type=MESH)
    for d in range(1, npeer):
        pl.semaphore_signal(barrier, inc=1, device_id=pdev(ppeer(d)), device_id_type=MESH)
    for d in range(1, ny):
        pl.semaphore_signal(barrier, inc=1, device_id=ydev(ypeer(d)), device_id_type=MESH)
    pl.semaphore_wait(barrier, nz + npeer + ny - 3)

    meta_copies = [
        remote(meta_ref, metaz.at[z], m_s.at[d], m_r.at[d], zdev(zpeer(d))) for d in range(1, nz)
    ]
    w_copies = [
        remote(w_ref, wfull.at[y], w_s.at[d], w_r.at[d], ydev(ypeer(d))) for d in range(1, ny)
    ]
    w_local = pltpu.make_async_copy(w_ref, wfull.at[y], loc.at[0])
    w_local.start()

    def z_in(u, src):
        pltpu.make_async_copy(src.at[:, columns(z)], zbuf.at[u, z], zin_r.at[u, 0]).start()
        return [
            remote(
                src.at[:, columns(zpeer(d))], zbuf.at[u, z], zin_s.at[u, d], zin_r.at[u, d],
                zdev(zpeer(d)),
            )
            for d in range(1, nz)
        ]

    zin_copies = [z_in(0, q_ref), z_in(1, k_ref), z_in(2, v_ref)]
    metaz[z] = meta_ref[...]

    w_local.wait()
    for copy in w_copies:
        copy.wait_recv()
    wrows = wfull.shape[1]

    def dz_block(i, _):
        r = pl.ds(pl.multiple_of(i * 128, 128), 128)
        cot = cot_ref[r, :]
        for j in range(ny):
            c = slice(j * wrows, (j + 1) * wrows)
            gg_ref[r, c] = (nt(cot, wfull[j]) * gates_ref[r, c].astype(F32)).astype(BF16)
        return 0

    lax.fori_loop(0, rows // 128, dz_block, 0)
    zin_copies.append(z_in(3, gg_ref))

    for copy in meta_copies:
        copy.wait_recv()
    for at in range(npeer):
        tsend[at] = metaz[:, at, 512:640]
    t_copies = [
        remote(tsend.at[ppeer(d)], trecv.at[p], t_s.at[d], t_r.at[d], pdev(ppeer(d)))
        for d in range(1, npeer)
    ]
    trecv[p] = tsend[p]

    def build_src(i, _):
        slot = metaz[i, 0:1, 0:512]
        for c in range(slots // 128):
            ids = lax.broadcasted_iota(jnp.int32, (128, rows), 0) + c * 128
            onehot_src[i, c * 128 : (c + 1) * 128, :] = jnp.where(ids == slot, 1.0, 0.0).astype(BF16)
        return 0

    lax.fori_loop(0, nz, build_src, 0)

    def pack_in(u):
        def step(d, _):
            at = lax.rem(z - d + nz, nz)
            block_wait(zbuf.at[u, at], zin_r.at[u, d])
            moved = nn(onehot_src[at], zbuf[u, at]).astype(BF16)
            xsend[u, :, :, at] = moved.reshape(npeer, nz, SLOTS, HEAD)
            return 0

        lax.fori_loop(0, nz, step, 0)
        pltpu.make_async_copy(xsend.at[u, p], xrecv.at[u, p], xin_r.at[u, 0]).start()
        return [
            remote(
                xsend.at[u, ppeer(d)], xrecv.at[u, p], xin_s.at[u, d], xin_r.at[u, d],
                pdev(ppeer(d)),
            )
            for d in range(1, npeer)
        ]

    def unpack_in(u):
        for d in range(npeer):
            at = lax.rem(p - d + npeer, npeer)
            block_wait(xrecv.at[u, at], xin_r.at[u, d])

        def step(o, _):
            own[u, o] = nn(onehot_own[o], xrecv[u, :, o].reshape(slots, HEAD)).astype(BF16)
            return 0

        lax.fori_loop(0, nz, step, 0)

    xin_copies = [pack_in(0)]

    for copy in t_copies:
        copy.wait_recv()
    group = npeer * nz

    def build_own(o, _):
        table = trecv[...].reshape(group, 128)
        high = (table // 16).astype(F32).astype(BF16)
        low = (table % 16).astype(F32).astype(BF16)
        lane = lax.broadcasted_iota(jnp.int32, (128, slots), 1)
        take = lax.broadcasted_iota(jnp.int32, (128, slots), 0)
        pick = jnp.where(take == o * SLOTS + lane % SLOTS, 1.0, 0.0).astype(BF16)
        spread = nn(high, pick) * 16.0 + nn(low, pick)
        which = lax.broadcasted_iota(jnp.int32, (group, slots), 0)
        at = lax.broadcasted_iota(jnp.int32, (group, slots), 1) // SLOTS
        row = jnp.sum(jnp.where(which == at, spread, 0.0), axis=0, keepdims=True).astype(jnp.int32)
        for c in range(rows // 128):
            ids = lax.broadcasted_iota(jnp.int32, (128, slots), 0) + c * 128
            onehot_own[o, c * 128 : (c + 1) * 128, :] = jnp.where(ids == row, 1.0, 0.0).astype(BF16)
        return 0

    lax.fori_loop(0, nz, build_own, 0)

    xin_copies.append(pack_in(1))
    unpack_in(0)
    xin_copies.append(pack_in(2))
    unpack_in(1)
    xin_copies.append(pack_in(3))
    unpack_in(2)

    def allowed_of(o):
        lengths = metaz[o, 0:1, 640:768]
        line = lax.broadcasted_iota(jnp.int32, (rows, 1), 0)
        end = jnp.zeros((1, 1), jnp.int32)
        start = jnp.zeros((rows, 1), jnp.int32)
        for h in range(8):
            length = lengths[:, h : h + 1]
            end = end + length
            start = start + jnp.where(line >= end, length, 0)
        i = lax.broadcasted_iota(jnp.int32, (rows, rows), 0)
        j = lax.broadcasted_iota(jnp.int32, (rows, rows), 1)
        return (j <= i) & (j >= start)

    for copy in xin_copies[0]:
        copy.wait_send()

    def forward(o, _):
        scores = nt(own[0, o], own[1, o]) * scale
        sig = 0.5 * jnp.tanh(0.5 * scores) + 0.5
        weights = jnp.where(allowed_of(o), scores * sig, 0.0).astype(BF16)
        att = nn(weights, own[2, o]).astype(BF16)
        att_own[o] = att
        moved = tn(att, onehot_own[o]).T.astype(BF16)
        xsend[0, :, o] = moved.reshape(npeer, nz, SLOTS, HEAD)
        return 0

    lax.fori_loop(0, nz, forward, 0)

    def x_out(u):
        pltpu.make_async_copy(xsend.at[u, p], xback.at[u, p], xo_r.at[u, 0]).start()
        return [
            remote(
                xsend.at[u, ppeer(d)], xback.at[u, p], xo_s.at[u, d], xo_r.at[u, d],
                pdev(ppeer(d)),
            )
            for d in range(1, npeer)
        ]

    xo_copies = [x_out(0)]

    unpack_in(3)

    def stats(o, _):
        att = att_own[o].astype(F32)
        dz = own[3, o].astype(F32)
        mean = jnp.sum(att, axis=1, keepdims=True) * (1.0 / HEAD)
        cent = att - mean
        second = jnp.sum(cent * cent, axis=1, keepdims=True)
        total = jnp.sum(dz, axis=1, keepdims=True)
        cross = jnp.sum(dz * cent, axis=1, keepdims=True)
        lane = lax.broadcasted_iota(jnp.int32, (rows, HEAD), 1)
        table = jnp.where(
            lane == 0, mean, jnp.where(lane == 1, second, jnp.where(lane == 2, total, cross))
        )
        stat_s[o] = table.T[0:8, :]
        return 0

    lax.fori_loop(0, nz, stats, 0)
    sa_copies = [
        remote(stat_s.at[zpeer(d)], stat_r.at[z], sa_s.at[d], sa_r.at[d], zdev(zpeer(d)))
        for d in range(1, nz)
    ]
    stat_r[z] = stat_s[z]
    for copy in sa_copies:
        copy.wait_recv()
    features = float(nz * HEAD)
    got = stat_r[...]
    means, seconds, totals, crosses = [got[:, i : i + 1, :] for i in range(4)]
    mean = jnp.sum(means, axis=0) * (1.0 / nz)
    shift = means - mean[None]
    var = (jnp.sum(seconds, axis=0) + HEAD * jnp.sum(shift * shift, axis=0)) / features
    inverse = lax.rsqrt(var + EPSILON)
    mean_grad = jnp.sum(totals, axis=0) / features
    mean_cross = jnp.sum(crosses + shift * totals, axis=0) * inverse / features
    stat_f[z] = jnp.concatenate([mean, inverse, mean_grad, mean_cross] * 2, axis=0)
    sb_copies = [
        remote(stat_f.at[z], stat_f.at[z], sb_s.at[d], sb_r.at[d], zdev(zpeer(d)))
        for d in range(1, nz)
    ]
    for u in (1, 2, 3):
        for copy in xin_copies[u]:
            copy.wait_send()
    for copy in sb_copies:
        copy.wait_recv()

    def backward(o, _):
        full = jnp.concatenate([stat_f[o]] * (HEAD // 8), axis=0).T
        mean, inverse = full[:, 0:1], full[:, 1:2]
        mean_grad, mean_cross = full[:, 2:3], full[:, 3:4]
        normed = (att_own[o].astype(F32) - mean) * inverse
        grad = (own[3, o].astype(F32) - mean_grad - normed * mean_cross) * inverse
        grad = grad.astype(BF16)
        allowed = allowed_of(o)
        q, k, v = own[0, o], own[1, o], own[2, o]
        scores = nt(q, k) * scale
        sig = 0.5 * jnp.tanh(0.5 * scores) + 0.5
        value = scores * sig
        weights = jnp.where(allowed, value, 0.0).astype(BF16)
        probs = nt(grad, v)
        slope = sig + value * (1.0 - sig)
        gs = jnp.where(allowed, probs * slope * scale, 0.0).astype(BF16)
        gq_t = nn(gs, k).astype(BF16)
        gk_t = tn(q, gs).astype(BF16)
        gv_t = tn(grad, weights).astype(BF16)
        spots = onehot_own[o]
        xsend[1, :, o] = tn(gq_t, spots).T.astype(BF16).reshape(npeer, nz, SLOTS, HEAD)
        xsend[2, :, o] = nn(gk_t, spots).T.astype(BF16).reshape(npeer, nz, SLOTS, HEAD)
        xsend[3, :, o] = nn(gv_t, spots).T.astype(BF16).reshape(npeer, nz, SLOTS, HEAD)
        return 0

    lax.fori_loop(0, nz, backward, 0)
    xo_copies += [x_out(1), x_out(2), x_out(3)]
    for u in range(4):
        for copy in zin_copies[u]:
            copy.wait_send()

    def back(u, dst):
        for d in range(npeer):
            at = lax.rem(p - d + npeer, npeer)
            block_wait(xback.at[u, at], xo_r.at[u, d])
        stage = pltpu.make_async_copy(xback.at[u], xrecv.at[u], loc.at[1 + u])
        stage.start()
        stage.wait()

        def tokens(at):
            got = xrecv[u, :, :, at].reshape(slots, HEAD)
            zbuf[u, at] = tn(got, onehot_src[at]).T.astype(BF16)

        def step(d, _):
            at = lax.rem(z + d, nz)
            tokens(at)
            remote(
                zbuf.at[u, at], dst.at[:, columns(z)], zo_s.at[u, d], zo_r.at[u, d], zdev(at)
            )
            return 0

        lax.fori_loop(1, nz, step, 0)
        tokens(z)
        pltpu.make_async_copy(zbuf.at[u, z], dst.at[:, columns(z)], zo_r.at[u, 0]).start()

    def back_wait(u, dst):
        for d in range(nz):
            at = lax.rem(z - d + nz, nz)
            block_wait(dst.at[:, columns(at)], zo_r.at[u, d])

    back(0, att_full)
    back(1, gq_ref)

    back_wait(0, att_full)

    def final_block(i, _):
        r = pl.ds(pl.multiple_of(i * 128, 128), 128)
        att = att_full[r, :].astype(F32)
        cent = att - jnp.mean(att, axis=1, keepdims=True)
        inv = lax.rsqrt(jnp.mean(cent * cent, axis=1, keepdims=True) + EPSILON)
        normed = cent * inv
        gated = (normed * gates_ref[r, :].astype(F32)).astype(BF16)
        att_full[r, :] = gated
        cot = cot_ref[r, :]
        acc = None
        for j in range(ny):
            c = slice(j * wrows, (j + 1) * wrows)
            gg_ref[r, c] = (nt(cot, wfull[j]) * normed[:, c]).astype(BF16)
            part = nn(gated[:, c], wfull[j])
            acc = part if acc is None else acc + part
        out_ref[r, :] = acc.astype(BF16)
        return 0

    lax.fori_loop(0, rows // 128, final_block, 0)

    def weight_block(j, _):
        c = pl.ds(pl.multiple_of(j * wrows, wrows), wrows)
        dw_send[j] = tn(att_full[:, c], cot_ref[...]).astype(BF16)
        return 0

    lax.fori_loop(0, ny, weight_block, 0)
    dy_copies = [
        remote(dw_send.at[ypeer(d)], dw_recv.at[y], dy_s.at[d], dy_r.at[d], ydev(ypeer(d)))
        for d in range(1, ny)
    ]
    back(2, gk_ref)
    dw_recv[y] = dw_send[y]
    for copy in dy_copies:
        copy.wait_recv()
    part = wrows // npeer

    def sum_y(j, _):
        r = pl.ds(pl.multiple_of(j * part, part), part)
        acc = dw_recv[0, r, :].astype(F32)
        for i in range(1, ny):
            acc = acc + dw_recv[i, r, :].astype(F32)
        r1_send[j] = acc.astype(BF16)
        return 0

    lax.fori_loop(0, npeer, sum_y, 0)
    dp_copies = [
        remote(r1_send.at[ppeer(d)], r1_recv.at[p], dp_s.at[d], dp_r.at[d], pdev(ppeer(d)))
        for d in range(1, npeer)
    ]
    back(3, gv_ref)
    r1_recv[p] = r1_send[p]
    for copy in dp_copies:
        copy.wait_recv()
    acc = r1_recv[0].astype(F32)
    for i in range(1, npeer):
        acc = acc + r1_recv[i].astype(F32)
    for i in range(nz):
        r2_send[i] = acc[:, i * HEAD : (i + 1) * HEAD].astype(BF16)
    dz_copies = [
        remote(r2_send.at[zpeer(d)], r2_recv.at[z], dz_s.at[d], dz_r.at[d], zdev(zpeer(d)))
        for d in range(1, nz)
    ]
    r2_recv[z] = r2_send[z]
    for copy in dz_copies:
        copy.wait_recv()
    acc = r2_recv[0].astype(F32)
    for i in range(1, nz):
        acc = acc + r2_recv[i].astype(F32)
    gz[z] = acc.astype(BF16)
    az_copies = [
        remote(gz.at[z], gz.at[z], az_s.at[d], az_r.at[d], zdev(zpeer(d))) for d in range(1, nz)
    ]
    for copy in az_copies:
        copy.wait_recv()
    gp[p] = jnp.concatenate([gz[i] for i in range(nz)], axis=1)
    ap_copies = [
        remote(gp.at[p], gp.at[p], ap_s.at[d], ap_r.at[d], pdev(ppeer(d)))
        for d in range(1, npeer)
    ]
    for copy in ap_copies:
        copy.wait_recv()
    gw_ref[...] = gp[...].reshape(wrows, gw_ref.shape[1]).astype(F32)

    for u, dst in ((1, gq_ref), (2, gk_ref), (3, gv_ref)):
        back_wait(u, dst)
    for u in range(4):
        for d in range(1, nz):
            block_wait(zbuf.at[u, zpeer(d)], zo_s.at[u, d])
        for copy in xo_copies[u]:
            copy.wait_send()
    for copies in (
        meta_copies, w_copies, t_copies, sa_copies, sb_copies,
        dy_copies, dp_copies, dz_copies, az_copies, ap_copies,
    ):
        for copy in copies:
            copy.wait_send()


def slot_tables(hist_len, token_owner, token_row, nz, npeer):
    rows = token_owner.shape[0]
    owners = nz * npeer
    match = token_owner[:, None] == jnp.arange(owners, dtype=jnp.int32)[None, :]
    before = jnp.arange(rows)[:, None] > jnp.arange(rows)[None, :]
    earlier = jnp.dot(before.astype(BF16), match.astype(BF16), preferred_element_type=F32)
    rank = jnp.sum(jnp.where(match, earlier, 0.0), axis=1).astype(jnp.int32)
    slot = lax.rem(token_owner, npeer) * (nz * SLOTS) + (token_owner // npeer) * SLOTS + rank
    at = slot[:, None] == jnp.arange(owners * SLOTS, dtype=jnp.int32)[None, :]
    row_of = jnp.min(jnp.where(at, token_row[:, None], rows), axis=0).reshape(npeer, nz * SLOTS)
    spread = jnp.broadcast_to(slot[None, :], (8, rows))
    lengths = jnp.broadcast_to(jnp.pad(hist_len, ((0, 0), (0, 120))), (8, 128))
    return jnp.concatenate([spread, row_of, lengths], axis=1)


def body(nz, npeer, ny, queries, keys, values, gates, cotangent, hist_len, token_owner, token_row, w_out):
    rows, width = queries.shape
    meta = slot_tables(hist_len, token_owner, token_row, nz, npeer)
    slots = nz * npeer * SLOTS
    wrows = w_out.shape[0]
    part = wrows // npeer
    dma = pltpu.SemaphoreType.DMA
    vmem = pl.BlockSpec(memory_space=pltpu.VMEM)
    anywhere = pl.BlockSpec(memory_space=pl.ANY)
    wide = jax.ShapeDtypeStruct((rows, width), BF16)
    out = pl.pallas_call(
        functools.partial(kernel, nz, npeer, ny),
        out_shape=(
            wide, wide, wide, wide, wide,
            jax.ShapeDtypeStruct((wrows, width), F32),
            jax.ShapeDtypeStruct((4, npeer, nz, nz, SLOTS, HEAD), BF16),
        ),
        in_specs=[anywhere, anywhere, anywhere, vmem, vmem, vmem, anywhere],
        out_specs=(vmem, anywhere, anywhere, anywhere, vmem, vmem, anywhere),
        scratch_shapes=[
            pltpu.VMEM((nz, slots, rows), BF16),
            pltpu.VMEM((nz, rows, slots), BF16),
            pltpu.VMEM((4, nz, rows, HEAD), BF16),
            pltpu.VMEM((4, npeer, nz, nz, SLOTS, HEAD), BF16),
            pltpu.VMEM((4, npeer, nz, nz, SLOTS, HEAD), BF16),
            pltpu.VMEM((4, nz, rows, HEAD), BF16),
            pltpu.VMEM((nz, rows, HEAD), BF16),
            pltpu.VMEM((ny, wrows, width), BF16),
            pltpu.VMEM((rows, width), BF16),
            pltpu.VMEM((nz, 8, META), jnp.int32),
            pltpu.VMEM((npeer, nz, 128), jnp.int32),
            pltpu.VMEM((npeer, nz, 128), jnp.int32),
            pltpu.VMEM((nz, 8, rows), F32),
            pltpu.VMEM((nz, 8, rows), F32),
            pltpu.VMEM((nz, 8, rows), F32),
            pltpu.VMEM((ny, wrows, width), BF16),
            pltpu.VMEM((ny, wrows, width), BF16),
            pltpu.VMEM((npeer, part, width), BF16),
            pltpu.VMEM((npeer, part, width), BF16),
            pltpu.VMEM((nz, part, HEAD), BF16),
            pltpu.VMEM((nz, part, HEAD), BF16),
            pltpu.VMEM((nz, part, HEAD), BF16),
            pltpu.VMEM((npeer, part, width), BF16),
            dma((5,)),
            dma((4, nz)), dma((4, nz)),
            dma((4, npeer)), dma((4, npeer)),
            dma((4, npeer)), dma((4, npeer)),
            dma((4, nz)), dma((4, nz)),
            dma((nz,)), dma((nz,)),
            dma((npeer,)), dma((npeer,)),
            dma((ny,)), dma((ny,)),
            dma((nz,)), dma((nz,)),
            dma((nz,)), dma((nz,)),
            dma((ny,)), dma((ny,)),
            dma((npeer,)), dma((npeer,)),
            dma((nz,)), dma((nz,)),
            dma((nz,)), dma((nz,)),
            dma((npeer,)), dma((npeer,)),
        ],
        compiler_params=pltpu.CompilerParams(
            collective_id=0, has_side_effects=True, vmem_limit_bytes=63 * 1024 * 1024
        ),
    )(queries, keys, values, gates, cotangent, meta, w_out)
    return out[:6]


def solution(mesh):
    ny = mesh.shape["dp"]
    nz = 8
    npeer = mesh.shape["bal"] // nz
    token = P(("dp", "bal"))
    wide = P(("dp", "bal"), None)
    return jax.shard_map(
        functools.partial(body, nz, npeer, ny),
        mesh=mesh,
        in_specs=(wide, wide, wide, wide, wide, wide, token, token, P("dp", None)),
        out_specs=(wide, wide, wide, wide, wide, P("dp", None)),
        check_vma=False,
    )
```

time: 856 us -> 297 us (0.35); the launches traced: 843 us -> 296 us
  blocking collectives: 400 us -> 0 us
  Pallas kernels: 0 us -> 284 us
  waiting for transfers between devices: 221 us -> 0 us
  local copies, waits for them, and re-layouts: 89.4 us -> 7.95 us
  starting transfers between devices: 55.9 us -> 0 us
  matrix products: 36.5 us -> 1.04 us
  other arithmetic: 25.1 us -> 2.36 us
  between operations: 14.9 us -> 0.68 us
    psum x1 -> x0, blocking collectives: 286 us -> none  [weight_grads(): return lax.psum(group_share, 'bal')]
    pallas_call x0 -> x1, Pallas kernels: none -> 284 us  [body(): pl.pallas_call(functools.partial(kernel, nz, npeer, ny), out_shape=(wide,...]
    all_to_all x7 -> x0, waiting for transfers between devices: 221 us -> none  [the longest x1 48.9 us: body(): lax.all_to_all(to_slots(attended_own, landing), 'bal', split_axis=0, conc...]
    all_to_all x2 -> x0, blocking collectives: 113 us -> none  [the longest x1 56.8 us: body(): lax.all_to_all(pack(grad_attended, 0), 'bal', split_axis=0, concat_axis=0...]
    all_to_all x7 -> x0, starting transfers between devices: 55.7 us -> none  [the longest x1 13 us: body(): lax.all_to_all(pack(token_row, row_count), 'bal', split_axis=0, concat_ax...]
    scatter x9 -> x0, local copies, waits for them, and re-layouts: 43.6 us -> none  [the longest x5 26.6 us: unpack_owner(): jnp.zeros((row_count,) + flat.shape[1:], flat.dtype).at[landing]]
    gather x8 -> x0, local copies, waits for them, and re-layouts: 37 us -> none  [the longest x4 21.5 us: to_slots(): jnp.take(tensor, jnp.minimum(landing, row_count - 1), axis=0)]
    dot_general x9 -> x1, matrix products: 36.5 us -> 1.04 us  [slot_tables(): jnp.dot(before.astype(BF16), match.astype(BF16), preferred_element_type=F32)]
  transfers between devices with their start and end apart: 9 -> 0, of which waited for: 6 -> 0; matrix products, arithmetic and copies ran while one was open for 6% -> 0% of each run, Pallas kernels for 0% -> 0%
where the time goes in v1:
time: 297 us; the launch traced here: 296 us
  Pallas kernels  284 us (96%)
  local copies, waits for them, and re-layouts  7.95 us (3%)
    pallas_call x1, Pallas kernels, body(): pl.pallas_call(functools.partial(kernel, nz, npeer, ny), out_shape=(wide,...  284 us
    unnamed x16, local copies, waits for them, and re-layouts  7.28 us

profile of v1, /device:TPU:1, one launch (start us, length us, event | category | flops | bytes accessed | tf_op | source)
XLA Modules:
  0.0 296.2 jit_solution(15188724028290415492)
XLA Ops:
  0.6 0.7 pad_bitcast_fusion
  1.3 1.0 fusion
  2.3 0.7 fusion.4
  3.0 1.0 select_reduce_fusion
  4.1 0.6 add_add_fusion.meta_ref
  4.7 284.1 %shard_map.136 = (bf16[512,1024]{1,0:T(8,128)(2,1)}, bf16[512,1024]{1,0:T(8,128)(2,1)}, bf16[512,1024]{1,0:T(8,128)(2,1)}, bf16[512,1024]{1,0:T(8,128)(2,1)}, bf...) custom-call(bf16[512,1024]{1,0:T(8,128)(2,1)} %q_ref.1, ...), custom_call_target="tpu_custom_call" | custom-call | tf_op jit(solution)/shard_map/pallas_call | solution.py:483
  288.9 0.0 copy-start.4
  288.9 0.0 copy-start.3
  288.9 2.4 copy.21
  291.3 0.0 copy-done.4
  291.3 0.0 copy-start.2
  291.3 1.0 copy.22
  292.3 0.0 copy-done.3
  292.3 0.0 copy-start.1
  292.3 1.0 copy.23
  293.2 0.0 copy-done.2
  293.2 0.0 copy-start
  293.2 1.0 copy.24
  294.2 0.0 copy-done.1
  294.2 1.0 copy.25
  295.2 0.0 copy-done
  295.2 1.0 copy.26
  (2 shorter events, 0.0 us)
Async XLA Ops:
  288.9 2.4 copy-start.4
  288.9 3.4 %copy-start.3 = (bf16[512,1024]{1,0:T(8,128)(2,1)S(1)}, bf16[512,1024]{1,0:T(8,128)(2,1)}, u32[]{:S(2)}) copy-start(bf16[512,1024]{1,0:T(8,128)(2,1)} %get-tuple-element.26) | copy-start | bytes 3145732
  291.3 1.9 copy-start.2
  292.3 1.9 copy-start.1
  293.2 1.9 copy-start

commit v2 on v1

v2 whole, which is shorter than its diff:
```python
import functools
import math

import jax
import jax.numpy as jnp
from jax import lax
from jax.experimental import pallas as pl
from jax.experimental.pallas import tpu as pltpu
from jax.sharding import PartitionSpec as P

HEAD = 128
EPSILON = 1e-05
SLOTS = 16
MESH = pl.DeviceIdType.MESH
F32 = jnp.float32
BF16 = jnp.bfloat16
META = 768


def nn(a, b):
    return lax.dot_general(a, b, (((1,), (0,)), ((), ())), preferred_element_type=F32)


def nt(a, b):
    return lax.dot_general(a, b, (((1,), (1,)), ((), ())), preferred_element_type=F32)


def tn(a, b):
    return lax.dot_general(a, b, (((0,), (0,)), ((), ())), preferred_element_type=F32)


def block_wait(ref, sem):
    pltpu.make_async_copy(ref, ref, sem).wait()


def kernel(
    nz, npeer, ny,
    q_ref, k_ref, v_ref, gates_ref, cot_ref, owner_ref, row_ref, len_ref, w_ref,
    out_to, gq_ref, gk_ref, gv_ref, gg_to, gw_ref,
    out_ref, gg_ref, onehot_src, onehot_own, zbuf, xsend, xrecv, own, att_own, wbuf, wfull, att_full,
    metaz, hist, tsend, trecv, stat_s, stat_r, stat_f,
    pair_recv, dw_recv, r1_send, r1_recv, r2_send, r2_recv, gz,
    loc, zin_s, zin_r, xin_s, xin_r, xo_s, xo_r, zo_s, zo_r,
    m_s, m_r, t_s, t_r, w_s, w_r, sa_s, sa_r, sb_s, sb_r,
    pr_s, pr_r, dy_s, dy_r, dp_s, dp_r, dz_s, dz_r, az_s, az_r, ap_s, ap_r,
):
    y = lax.axis_index("dp")
    b = lax.axis_index("bal")
    z = b // npeer
    p = lax.rem(b, npeer)
    rows = q_ref.shape[0]
    wrows = wfull.shape[1]
    part = wrows // npeer
    half = rows // 2
    slots = npeer * nz * SLOTS
    scale = 1.0 / math.sqrt(HEAD)
    order = [0]
    for d in range(1, nz // 2 + 1):
        order += [d, nz - d] if 2 * d < nz else [d]
    chunks = 4
    per = nz // chunks
    bounds = (0, 1, 2, 4, 6, 8)

    def zpeer(d):
        return lax.rem(z + d, nz)

    def ppeer(d):
        return lax.rem(p + d, npeer)

    def ypeer(d):
        return lax.rem(y + d, ny)

    def zdev(at):
        return (y, at * npeer + p)

    def pdev(at):
        return (y, z * npeer + at)

    def ydev(at):
        return (at, b)

    def columns(at):
        return pl.ds(pl.multiple_of(at * HEAD, HEAD), HEAD)

    def remote(src, dst, ssem, rsem, device):
        copy = pltpu.make_async_remote_copy(
            src_ref=src, dst_ref=dst, send_sem=ssem, recv_sem=rsem,
            device_id=device, device_id_type=MESH,
        )
        copy.start()
        return copy

    barrier = pltpu.get_barrier_semaphore()
    for d in range(1, nz):
        pl.semaphore_signal(barrier, inc=1, device_id=zdev(zpeer(d)), device_id_type=MESH)
    for d in range(1, npeer):
        pl.semaphore_signal(barrier, inc=1, device_id=pdev(ppeer(d)), device_id_type=MESH)
    for d in range(1, ny):
        pl.semaphore_signal(barrier, inc=1, device_id=ydev(ypeer(d)), device_id_type=MESH)

    owner = owner_ref[...]
    column = jnp.broadcast_to(owner.astype(F32), (128, rows)).T[:, 0:1]
    first = lax.broadcasted_iota(jnp.int32, (rows, rows), 0)
    second = lax.broadcasted_iota(jnp.int32, (rows, rows), 1)
    same = (column == owner.astype(F32)) & (first < second)
    rank = jnp.sum(jnp.where(same, 1.0, 0.0), axis=0, keepdims=True).astype(jnp.int32)
    slot = lax.rem(owner, npeer) * (nz * SLOTS) + lax.div(owner, npeer) * SLOTS + rank
    metaz[0, :, 0:rows] = jnp.broadcast_to(slot, (8, rows))

    def build_src(i, _):
        slot = metaz[i, 0:1, 0:rows]
        for c in range(slots // 128):
            ids = lax.broadcasted_iota(jnp.int32, (128, rows), 0) + c * 128
            onehot_src[i, c * 128 : (c + 1) * 128, :] = jnp.where(ids == slot, 1.0, 0.0).astype(BF16)
        return 0

    build_src(0, 0)
    token_row = jnp.broadcast_to(row_ref[...], (8, rows))
    line = lax.broadcasted_iota(jnp.int32, (8, rows), 0)
    digits = jnp.where(
        line == 0, lax.div(token_row, 16), jnp.where(line == 1, lax.rem(token_row, 16), 1)
    )
    found = nt(digits.astype(F32).astype(BF16), onehot_src[0])
    row_of = found[0:1] * 16.0 + found[1:2] + (1.0 - found[2:3]) * rows
    row_of = row_of.astype(jnp.int32)
    metaz[0, :, 512:640] = jnp.concatenate(
        [row_of[:, i * nz * SLOTS : (i + 1) * nz * SLOTS] for i in range(npeer)], axis=0
    )
    metaz[0, :, 640:768] = jnp.broadcast_to(len_ref[...], (8, 128))

    pl.semaphore_wait(barrier, nz + npeer + ny - 3)

    meta_copies = [
        remote(metaz.at[0], metaz.at[j], m_s.at[j], m_r.at[j], zdev(zpeer(order[j])))
        for j in range(1, nz)
    ]
    def z_in(u, src):
        pltpu.make_async_copy(src.at[:, columns(z)], zbuf.at[u, 0], zin_r.at[u, 0]).start()
        for j in range(1, nz):
            to = zpeer(order[j])
            remote(src.at[:, columns(to)], zbuf.at[u, j], zin_s.at[u], zin_r.at[u, j], zdev(to))

    z_in(0, q_ref)
    w_copies = [
        remote(w_ref, wfull.at[y], w_s.at[d], w_r.at[d], ydev(ypeer(d))) for d in range(1, ny)
    ]
    w_local = pltpu.make_async_copy(w_ref, wfull.at[y], loc.at[0])
    w_local.start()
    z_in(1, k_ref)
    z_in(2, v_ref)
    def pack_in(u, i):
        lo, hi = bounds[i], bounds[i + 1]
        places = slice(lo, hi)

        def step(j, _):
            block_wait(zbuf.at[u, j], zin_r.at[u, j])
            moved = nn(onehot_src[j], zbuf[u, j]).astype(BF16)
            xsend[u, :, :, j] = moved.reshape(npeer, nz, SLOTS, HEAD)
            return 0

        lax.fori_loop(lo, hi, step, 0)
        for d in range(1, npeer):
            to = ppeer(d)
            remote(
                xsend.at[u, to, :, places], xrecv.at[u, p, :, places], xin_s.at[u], xin_r.at[u],
                pdev(to),
            )
        if hi == nz:
            pltpu.make_async_copy(xsend.at[u, p], xrecv.at[u, p], xin_r.at[u]).start()

    def unpack_in(u):
        block_wait(xrecv.at[u], xin_r.at[u])

        def step(o, _):
            own[u, o] = nn(onehot_own[o], xrecv[u, :, o].reshape(slots, HEAD)).astype(BF16)
            return 0

        lax.fori_loop(0, nz, step, 0)

    for u in range(3):
        pack_in(u, 0)

    for copy in meta_copies:
        copy.wait_recv()
    for j in range(nz):
        hist[zpeer(nz - order[j])] = metaz[j, :, 640:768]
    for at in range(npeer):
        tsend[at] = metaz[:, at, 512:640]
    t_copies = [
        remote(tsend.at[ppeer(d)], trecv.at[p], t_s.at[d], t_r.at[d], pdev(ppeer(d)))
        for d in range(1, npeer)
    ]
    trecv[p] = tsend[p]
    lax.fori_loop(1, nz, build_src, 0)

    pack_in(0, 1)

    for copy in t_copies:
        copy.wait_recv()
    group = npeer * nz

    def build_own(o, _):
        table = trecv[...].reshape(group, 128)
        high = (table // 16).astype(F32).astype(BF16)
        low = (table % 16).astype(F32).astype(BF16)
        lane = lax.broadcasted_iota(jnp.int32, (128, slots), 1)
        take = lax.broadcasted_iota(jnp.int32, (128, slots), 0)
        pick = jnp.where(take == o * SLOTS + lane % SLOTS, 1.0, 0.0).astype(BF16)
        spread = nn(high, pick) * 16.0 + nn(low, pick)
        which = lax.broadcasted_iota(jnp.int32, (group, slots), 0)
        at = lax.broadcasted_iota(jnp.int32, (group, slots), 1) // SLOTS
        row = jnp.sum(jnp.where(which == at, spread, 0.0), axis=0, keepdims=True).astype(jnp.int32)
        for c in range(rows // 128):
            ids = lax.broadcasted_iota(jnp.int32, (128, slots), 0) + c * 128
            onehot_own[o, c * 128 : (c + 1) * 128, :] = jnp.where(ids == row, 1.0, 0.0).astype(BF16)
        return 0

    lax.fori_loop(0, nz, build_own, 0)

    def allowed_of(o):
        lengths = hist[o, 0:1, :]
        line = lax.broadcasted_iota(jnp.int32, (rows, 1), 0)
        end = jnp.zeros((1, 1), jnp.int32)
        start = jnp.zeros((rows, 1), jnp.int32)
        for h in range(8):
            length = lengths[:, h : h + 1]
            end = end + length
            start = start + jnp.where(line >= end, length, 0)
        i = lax.broadcasted_iota(jnp.int32, (rows, rows), 0)
        j = lax.broadcasted_iota(jnp.int32, (rows, rows), 1)
        return (j <= i) & (j >= start)

    def weigh(o, _):
        scores = nt(own[0, o], own[1, o]) * scale
        sig = 0.5 * jnp.tanh(0.5 * scores) + 0.5
        weights = jnp.where(allowed_of(o), scores * sig, 0.0).astype(BF16)
        wbuf[o, :, 0:rows] = weights[0:half]
        wbuf[o, :, rows:] = weights[half:]
        return 0

    def weights_of(o):
        return jnp.concatenate([wbuf[o, :, 0:rows], wbuf[o, :, rows:]], axis=0)

    def attend(o, _):
        att = nn(weights_of(o), own[2, o]).astype(BF16)
        att_own[o] = att
        moved = tn(att, onehot_own[o]).astype(BF16).T
        xsend[0, :, o] = moved.reshape(npeer, nz, SLOTS, HEAD)
        return 0

    def sent_in(u):
        block_wait(xsend.at[u, 1:npeer], xin_s.at[u])

    for i in range(2, 5):
        pack_in(0, i)
    pack_in(1, 1)
    pack_in(1, 2)

    w_local.wait()
    for copy in w_copies:
        copy.wait_recv()

    def dz_block(i, _):
        r = pl.ds(pl.multiple_of(i * 128, 128), 128)
        cot = cot_ref[r, :]
        for j in range(ny):
            c = slice(j * wrows, (j + 1) * wrows)
            gg_ref[r, c] = (nt(cot, wfull[j]) * gates_ref[r, c].astype(F32)).astype(BF16)
        return 0

    lax.fori_loop(0, rows // 128, dz_block, 0)
    z_in(3, gg_ref)

    unpack_in(0)
    pack_in(1, 3)
    pack_in(1, 4)
    pack_in(3, 0)
    pack_in(2, 1)
    pack_in(2, 2)
    unpack_in(1)
    pack_in(2, 3)
    lax.fori_loop(0, nz // 2, weigh, 0)
    pack_in(2, 4)
    lax.fori_loop(nz // 2, nz, weigh, 0)
    pack_in(3, 1)
    pack_in(3, 2)
    unpack_in(2)
    pack_in(3, 3)
    sent_in(0)
    lax.fori_loop(0, nz // 2, attend, 0)
    pack_in(3, 4)
    lax.fori_loop(nz // 2, nz, attend, 0)

    into = (0, 1, 2, 4)

    def x_out(u, parts=(3, 2, 1, 0), owners=slice(0, nz)):
        for i in parts:
            places = slice(i * per, (i + 1) * per)
            for d in range(1, npeer):
                to = ppeer(d)
                remote(
                    xsend.at[u, to, owners, places], xrecv.at[into[u], p, owners, places],
                    xo_s.at[u], xo_r.at[u, i], pdev(to),
                )
            pltpu.make_async_copy(
                xsend.at[u, p, owners, places], xrecv.at[into[u], p, owners, places],
                xo_r.at[u, i],
            ).start()

    def back(u, dst, i):
        places = slice(i * per, (i + 1) * per)
        block_wait(xrecv.at[into[u], :, :, places], xo_r.at[u, i])

        def tokens(j, _):
            got = xrecv[into[u], :, :, j].reshape(slots, HEAD)
            zbuf[u, j] = tn(got, onehot_src[j]).astype(BF16).T
            return 0

        lax.fori_loop(i * per, (i + 1) * per, tokens, 0)
        for j in range(i * per, (i + 1) * per):
            if j == 0:
                pltpu.make_async_copy(zbuf.at[u, 0], dst.at[:, columns(z)], zo_r.at[u]).start()
            else:
                remote(
                    zbuf.at[u, j], dst.at[:, columns(z)], zo_s.at[u], zo_r.at[u],
                    zdev(zpeer(nz - order[j])),
                )

    x_out(0, (0, 1, 3, 2))

    block_wait(xrecv.at[3], xin_r.at[3])

    def stats(o, _):
        moved = nn(onehot_own[o], xrecv[3, :, o].reshape(slots, HEAD)).astype(BF16)
        own[3, o] = moved
        att = att_own[o].astype(F32)
        dz = moved.astype(F32)
        mean = jnp.sum(att, axis=1, keepdims=True) * (1.0 / HEAD)
        cent = att - mean
        second = jnp.sum(cent * cent, axis=1, keepdims=True)
        total = jnp.sum(dz, axis=1, keepdims=True)
        cross = jnp.sum(dz * cent, axis=1, keepdims=True)
        lane = lax.broadcasted_iota(jnp.int32, (rows, HEAD), 1)
        table = jnp.where(
            lane == 0, mean, jnp.where(lane == 1, second, jnp.where(lane == 2, total, cross))
        )
        stat_s[o] = table.T[0:8, :]
        return 0

    lax.fori_loop(0, nz, stats, 0)
    sa_copies = [
        remote(stat_s.at[zpeer(d)], stat_r.at[z], sa_s.at[d], sa_r.at[d], zdev(zpeer(d)))
        for d in range(1, nz)
    ]
    stat_r[z] = stat_s[z]
    back(0, att_full, 0)
    for copy in sa_copies:
        copy.wait_recv()
    features = float(nz * HEAD)
    got = stat_r[...]
    means, seconds, totals, crosses = [got[:, i : i + 1, :] for i in range(4)]
    mean = jnp.sum(means, axis=0) * (1.0 / nz)
    shift = means - mean[None]
    var = (jnp.sum(seconds, axis=0) + HEAD * jnp.sum(shift * shift, axis=0)) / features
    inverse = lax.rsqrt(var + EPSILON)
    mean_grad = jnp.sum(totals, axis=0) / features
    mean_cross = jnp.sum(crosses + shift * totals, axis=0) * inverse / features
    stat_f[z] = jnp.concatenate([mean, inverse, mean_grad, mean_cross] * 2, axis=0)
    sb_copies = [
        remote(stat_f.at[z], stat_f.at[z], sb_s.at[d], sb_r.at[d], zdev(zpeer(d)))
        for d in range(1, nz)
    ]
    back(0, att_full, 1)
    for u in range(1, 4):
        sent_in(u)
    for copy in sb_copies:
        copy.wait_recv()

    def value_grads(o, _):
        full = jnp.concatenate([stat_f[o]] * (HEAD // 8), axis=0).T
        mean, inverse = full[:, 0:1], full[:, 1:2]
        mean_grad, mean_cross = full[:, 2:3], full[:, 3:4]
        normed = (att_own[o].astype(F32) - mean) * inverse
        grad = (own[3, o].astype(F32) - mean_grad - normed * mean_cross) * inverse
        grad = grad.astype(BF16)
        own[3, o] = grad
        gv_t = tn(grad, weights_of(o)).astype(BF16)
        xsend[1, :, o] = nn(gv_t, onehot_own[o]).astype(BF16).T.reshape(npeer, nz, SLOTS, HEAD)
        return 0

    def score_grads(o, _):
        q, k, v, grad = own[0, o], own[1, o], own[2, o], own[3, o]
        scores = nt(q, k) * scale
        sig = 0.5 * jnp.tanh(0.5 * scores) + 0.5
        slope = sig + scores * sig * (1.0 - sig)
        gs = jnp.where(allowed_of(o), nt(grad, v) * slope * scale, 0.0).astype(BF16)
        gq_t = nn(gs, k).astype(BF16)
        gk_t = tn(q, gs).astype(BF16)
        spots = onehot_own[o]
        xsend[2, :, o] = tn(gq_t, spots).astype(BF16).T.reshape(npeer, nz, SLOTS, HEAD)
        xsend[3, :, o] = nn(gk_t, spots).astype(BF16).T.reshape(npeer, nz, SLOTS, HEAD)
        return 0

    back(0, att_full, 3)
    lax.fori_loop(0, nz, value_grads, 0)
    x_out(1)
    back(0, att_full, 2)
    lax.fori_loop(0, 4, score_grads, 0)
    for u in range(4):
        block_wait(zbuf.at[u, 1:nz], zin_s.at[u])
    back(1, gv_ref, 3)
    lax.fori_loop(4, 6, score_grads, 0)
    back(1, gv_ref, 2)

    block_wait(att_full, zo_r.at[0])

    def final_block(i, _):
        r = pl.ds(pl.multiple_of(i * 128, 128), 128)
        att = att_full[r, :].astype(F32)
        cent = att - jnp.mean(att, axis=1, keepdims=True)
        inv = lax.rsqrt(jnp.mean(cent * cent, axis=1, keepdims=True) + EPSILON)
        normed = cent * inv
        gated = (normed * gates_ref[r, :].astype(F32)).astype(BF16)
        att_full[r, :] = gated
        cot = cot_ref[r, :]
        acc = None
        for j in range(ny):
            c = slice(j * wrows, (j + 1) * wrows)
            gg_ref[r, c] = (nt(cot, wfull[j]) * normed[:, c]).astype(BF16)
            step = nn(gated[:, c], wfull[j])
            acc = step if acc is None else acc + step
        out_ref[r, :] = acc.astype(BF16)
        return 0

    lax.fori_loop(0, rows // 128, final_block, 0)
    out_copy = pltpu.make_async_copy(out_ref, out_to, loc.at[1])
    out_copy.start()
    gg_copy = pltpu.make_async_copy(gg_ref, gg_to, loc.at[2])
    gg_copy.start()

    def weight_block(j, _):
        c = pl.ds(pl.multiple_of(j * wrows, wrows), wrows)
        wbuf[j] = tn(att_full[:, c], cot_ref[...]).astype(BF16)
        return 0

    lax.fori_loop(0, ny, weight_block, 0)
    core = lax.rem(p, 2)
    chip = lax.div(p, 2)
    chips = npeer // 2
    mine = pl.ds(pl.multiple_of(core * (wrows // 2), wrows // 2), wrows // 2)
    theirs = pl.ds(pl.multiple_of((1 - core) * (wrows // 2), wrows // 2), wrows // 2)
    pair = remote(
        wbuf.at[0:ny, theirs], pair_recv, pr_s.at[0], pr_r.at[0], pdev(chip * 2 + 1 - core)
    )
    lax.fori_loop(6, nz, score_grads, 0)
    x_out(2, (3, 2, 1))
    back(1, gv_ref, 1)
    pair.wait_recv()

    def sum_pair(j, _):
        wbuf[j, mine] = (wbuf[j, mine].astype(F32) + pair_recv[j].astype(F32)).astype(BF16)
        return 0

    lax.fori_loop(0, ny, sum_pair, 0)
    dy_copies = [
        remote(wbuf.at[ypeer(d), mine], dw_recv.at[y], dy_s.at[d], dy_r.at[d], ydev(ypeer(d)))
        for d in range(1, ny)
    ]
    dw_recv[y] = wbuf[y, mine]
    back(1, gv_ref, 0)
    back(2, gq_ref, 3)

    for copy in dy_copies:
        copy.wait_recv()

    def sum_y(j, _):
        r = pl.ds(pl.multiple_of(j * part, part), part)
        acc = dw_recv[0, r, :].astype(F32)
        for i in range(1, ny):
            acc = acc + dw_recv[i, r, :].astype(F32)
        r1_send[j] = acc.astype(BF16)
        return 0

    lax.fori_loop(0, chips, sum_y, 0)
    dp_copies = []
    for d in range(1, chips):
        to = lax.rem(chip + d, chips)
        dp_copies.append(
            remote(
                r1_send.at[to], r1_recv.at[chip], dp_s.at[d], dp_r.at[d], pdev(to * 2 + core)
            )
        )
    r1_recv[chip] = r1_send[chip]
    x_out(2, (0,))
    back(2, gq_ref, 2)
    for copy in dp_copies:
        copy.wait_recv()
    acc = r1_recv[0].astype(F32)
    for i in range(1, chips):
        acc = acc + r1_recv[i].astype(F32)
    for i in range(nz):
        r2_send[i] = acc[:, i * HEAD : (i + 1) * HEAD].astype(BF16)
    dz_copies = [
        remote(r2_send.at[zpeer(d)], r2_recv.at[z], dz_s.at[d], dz_r.at[d], zdev(zpeer(d)))
        for d in range(1, nz)
    ]
    r2_recv[z] = r2_send[z]
    x_out(3, (3, 2))
    back(2, gq_ref, 1)
    back(2, gq_ref, 0)
    for copy in dz_copies:
        copy.wait_recv()
    acc = r2_recv[0].astype(F32)
    for i in range(1, nz):
        acc = acc + r2_recv[i].astype(F32)
    gz[z] = acc.astype(BF16)
    az_copies = [
        remote(gz.at[z], gz.at[z], az_s.at[d], az_r.at[d], zdev(zpeer(d))) for d in range(1, nz)
    ]
    x_out(3, (1, 0))
    back(3, gk_ref, 3)
    back(3, gk_ref, 2)
    for copy in az_copies:
        copy.wait_recv()
    place = core * chips + chip
    gw_ref[place] = jnp.concatenate([gz[i] for i in range(nz)], axis=1)
    ap_copies = [
        remote(gw_ref.at[place], gw_ref.at[place], ap_s.at[d], ap_r.at[d], pdev(ppeer(d)))
        for d in range(1, npeer)
    ]
    back(3, gk_ref, 1)
    back(3, gk_ref, 0)
    for copy in ap_copies:
        copy.wait_recv()

    out_copy.wait()
    gg_copy.wait()
    for u, dst in ((1, gv_ref), (2, gq_ref), (3, gk_ref)):
        block_wait(dst, zo_r.at[u])
    for u in range(4):
        block_wait(zbuf.at[u, 1:nz], zo_s.at[u])
        block_wait(xsend.at[u, 1:npeer], xo_s.at[u])
    for copies in (
        meta_copies, w_copies, t_copies, sa_copies, sb_copies,
        [pair], dy_copies, dp_copies, dz_copies, az_copies, ap_copies,
    ):
        for copy in copies:
            copy.wait_send()


def settle(*refs):
    for src, dst in zip(refs[:5], refs[6:11]):
        dst[...] = src[...]
    refs[11][...] = refs[5][...].reshape(refs[11].shape).astype(F32)


def body(nz, npeer, ny, queries, keys, values, gates, cotangent, hist_len, token_owner, token_row, w_out):
    rows, width = queries.shape
    lengths = jnp.pad(hist_len, ((0, 0), (0, 120)))
    slots = nz * npeer * SLOTS
    wrows = w_out.shape[0]
    part = wrows // npeer
    dma = pltpu.SemaphoreType.DMA
    vmem = pl.BlockSpec(memory_space=pltpu.VMEM)
    anywhere = pl.BlockSpec(memory_space=pl.ANY)
    wide = jax.ShapeDtypeStruct((rows, width), BF16)
    out = pl.pallas_call(
        functools.partial(kernel, nz, npeer, ny),
        out_shape=(
            wide, wide, wide, wide, wide,
            jax.ShapeDtypeStruct((npeer, part, width), BF16),
        ),
        in_specs=[anywhere, anywhere, anywhere, vmem, vmem, vmem, vmem, vmem, anywhere],
        out_specs=(anywhere, anywhere, anywhere, anywhere, anywhere, vmem),
        scratch_shapes=[
            pltpu.VMEM((rows, width), BF16),
            pltpu.VMEM((rows, width), BF16),
            pltpu.VMEM((nz, slots, rows), BF16),
            pltpu.VMEM((nz, rows, slots), BF16),
            pltpu.VMEM((4, nz, rows, HEAD), BF16),
            pltpu.VMEM((4, npeer, nz, nz, SLOTS, HEAD), BF16),
            pltpu.VMEM((5, npeer, nz, nz, SLOTS, HEAD), BF16),
            pltpu.VMEM((4, nz, rows, HEAD), BF16),
            pltpu.VMEM((nz, rows, HEAD), BF16),
            pltpu.VMEM((nz, rows // 2, 2 * rows), BF16),
            pltpu.VMEM((ny, wrows, width), BF16),
            pltpu.VMEM((rows, width), BF16),
            pltpu.VMEM((nz, 8, META), jnp.int32),
            pltpu.VMEM((nz, 8, 128), jnp.int32),
            pltpu.VMEM((npeer, nz, 128), jnp.int32),
            pltpu.VMEM((npeer, nz, 128), jnp.int32),
            pltpu.VMEM((nz, 8, rows), F32),
            pltpu.VMEM((nz, 8, rows), F32),
            pltpu.VMEM((nz, 8, rows), F32),
            pltpu.VMEM((ny, wrows // 2, width), BF16),
            pltpu.VMEM((ny, wrows // 2, width), BF16),
            pltpu.VMEM((npeer // 2, part, width), BF16),
            pltpu.VMEM((npeer // 2, part, width), BF16),
            pltpu.VMEM((nz, part, HEAD), BF16),
            pltpu.VMEM((nz, part, HEAD), BF16),
            pltpu.VMEM((nz, part, HEAD), BF16),
            dma((3,)),
            dma((4,)), dma((4, nz)),
            dma((4,)), dma((4,)),
            dma((4,)), dma((4, 4)),
            dma((4,)), dma((4,)),
            dma((nz,)), dma((nz,)),
            dma((npeer,)), dma((npeer,)),
            dma((ny,)), dma((ny,)),
            dma((nz,)), dma((nz,)),
            dma((nz,)), dma((nz,)),
            dma((1,)), dma((1,)),
            dma((ny,)), dma((ny,)),
            dma((npeer // 2,)), dma((npeer // 2,)),
            dma((nz,)), dma((nz,)),
            dma((nz,)), dma((nz,)),
            dma((npeer,)), dma((npeer,)),
        ],
        compiler_params=pltpu.CompilerParams(
            collective_id=0, has_side_effects=True, vmem_limit_bytes=63 * 1024 * 1024
        ),
    )(
        queries, keys, values, gates, cotangent,
        token_owner.reshape(1, rows), token_row.reshape(1, rows), lengths, w_out,
    )
    out, gq, gk, gv, gg, gw = out
    steps = 4
    block = pl.BlockSpec((rows // steps, width), lambda i: (i, 0))
    gq, gk, gv, out, gg, gw = pl.pallas_call(
        settle,
        grid=(steps,),
        out_shape=(wide,) * 5 + (jax.ShapeDtypeStruct((wrows, width), F32),),
        in_specs=[block] * 5 + [pl.BlockSpec((npeer // steps, part, width), lambda i: (i, 0, 0))],
        out_specs=(block,) * 5 + (pl.BlockSpec((wrows // steps, width), lambda i: (i, 0)),),
        compiler_params=pltpu.CompilerParams(vmem_limit_bytes=60 * 1024 * 1024),
    )(gq, gk, gv, out, gg, gw)
    return out, gq, gk, gv, gg, gw


def solution(mesh):
    ny = mesh.shape["dp"]
    nz = 8
    npeer = mesh.shape["bal"] // nz
    token = P(("dp", "bal"))
    wide = P(("dp", "bal"), None)
    return jax.shard_map(
        functools.partial(body, nz, npeer, ny),
        mesh=mesh,
        in_specs=(wide, wide, wide, wide, wide, wide, token, token, P("dp", None)),
        out_specs=(wide, wide, wide, wide, wide, P("dp", None)),
        check_vma=False,
    )
```

time: 297 us -> 241 us (0.81)
  Pallas kernels: 284 us -> 239 us
  local copies, waits for them, and re-layouts: 7.95 us -> 1.16 us
    pallas_call x1, Pallas kernels: 284 us -> 234 us  [body(): pl.pallas_call(functools.partial(kernel, nz, npeer, ny), out_shape=(wide,...]
    unnamed x16 -> x2, local copies, waits for them, and re-layouts: 7.28 us -> 0.65 us
    pallas_call x0 -> x1, Pallas kernels: none -> 5.65 us  [body(): pl.pallas_call(settle, grid=(steps,), out_shape=(wide,) * 5 + (jax.ShapeD...]
where the time goes in v2:
time: 241 us
  Pallas kernels  239 us (99%)
    pallas_call x1, Pallas kernels, body(): pl.pallas_call(functools.partial(kernel, nz, npeer, ny), out_shape=(wide,...  234 us
    pallas_call x1, Pallas kernels, body(): pl.pallas_call(settle, grid=(steps,), out_shape=(wide,) * 5 + (jax.ShapeD...  5.65 us

profile of v2, /device:TPU:1, one launch (start us, length us, event | category | flops | bytes accessed | tf_op | source)
XLA Modules:
  0.0 241.2 jit_solution(3331275661201999988)
XLA Ops:
  0.6 0.0 copy-start
  0.6 0.6 copy-done
  1.3 0.5 pad.4.len_ref
  1.8 233.6 %shard_map.136 = (bf16[512,1024]{1,0:T(8,128)(2,1)}, bf16[512,1024]{1,0:T(8,128)(2,1)}, bf16[512,1024]{1,0:T(8,128)(2,1)}, bf16[512,1024]{1,0:T(8,128)(2,1)}, bf...) custom-call(bf16[512,1024]{1,0:T(8,128)(2,1)} %q_ref.1, bf16[512,1024]{1,0:T(8,128)(2,1)} %k_ref.1, ...), custom_call_target="tpu_custom_call" | custom-call | tf_op jit(solution)/shard_map/pallas_call | solution.py:567
  235.4 5.6 %shard_map.137 = (bf16[512,1024]{1,0:T(8,128)(2,1)}, bf16[512,1024]{1,0:T(8,128)(2,1)}, bf16[512,1024]{1,0:T(8,128)(2,1)}, bf16[512,1024]{1,0:T(8,128)(2,1)}, bf...) custom-call(bf16[512,1024]{1,0:T(8,128)(2,1)} %get-tuple-element.18.refs_0_, bf16[512,1024]{1,0:T(8,128)(2,1)} %get-tuple-element.19.refs_1_, ...), custom_call_target="tpu_custom_call" | custom-call | tf_op jit(solution)/shard_map/pallas_call | solution.py:629
Async XLA Ops:
  0.6 0.7 copy-start

commit v3 on v2

--- a/solution.py
+++ b/solution.py
@@ -57,9 +57,8 @@
     order = [0]
     for d in range(1, nz // 2 + 1):
         order += [d, nz - d] if 2 * d < nz else [d]
-    chunks = 4
-    per = nz // chunks
-    bounds = (0, 1, 2, 4, 6, 8)
+    bounds = (0, 1, 3, 5, 7, 8)
+    groups = ((0, 3), (3, 5), (5, 7), (7, 8))
 
     def zpeer(d):
         return lax.rem(z + d, nz)
@@ -126,7 +125,7 @@
     metaz[0, :, 512:640] = jnp.concatenate(
         [row_of[:, i * nz * SLOTS : (i + 1) * nz * SLOTS] for i in range(npeer)], axis=0
     )
-    metaz[0, :, 640:768] = jnp.broadcast_to(len_ref[...], (8, 128))
+    metaz[0, :, 640:648] = jnp.broadcast_to(len_ref[...], (8, 8))
 
     pl.semaphore_wait(barrier, nz + npeer + ny - 3)
 
@@ -295,7 +294,7 @@
 
     def x_out(u, parts=(3, 2, 1, 0), owners=slice(0, nz)):
         for i in parts:
-            places = slice(i * per, (i + 1) * per)
+            places = slice(*groups[i])
             for d in range(1, npeer):
                 to = ppeer(d)
                 remote(
@@ -308,16 +307,16 @@
             ).start()
 
     def back(u, dst, i):
-        places = slice(i * per, (i + 1) * per)
-        block_wait(xrecv.at[into[u], :, :, places], xo_r.at[u, i])
+        lo, hi = groups[i]
+        block_wait(xrecv.at[into[u], :, :, lo:hi], xo_r.at[u, i])
 
         def tokens(j, _):
             got = xrecv[into[u], :, :, j].reshape(slots, HEAD)
             zbuf[u, j] = tn(got, onehot_src[j]).astype(BF16).T
             return 0
 
-        lax.fori_loop(i * per, (i + 1) * per, tokens, 0)
-        for j in range(i * per, (i + 1) * per):
+        lax.fori_loop(lo, hi, tokens, 0)
+        for j in range(lo, hi):
             if j == 0:
                 pltpu.make_async_copy(zbuf.at[u, 0], dst.at[:, columns(z)], zo_r.at[u]).start()
             else:
@@ -326,7 +325,7 @@
                     zdev(zpeer(nz - order[j])),
                 )
 
-    x_out(0, (0, 1, 3, 2))
+    x_out(0, (3, 0, 1, 2))
 
     block_wait(xrecv.at[3], xin_r.at[3])
 
@@ -347,13 +346,14 @@
         stat_s[o] = table.T[0:8, :]
         return 0
 
-    lax.fori_loop(0, nz, stats, 0)
+    lax.fori_loop(0, nz // 2, stats, 0)
+    back(0, att_full, 3)
+    lax.fori_loop(nz // 2, nz, stats, 0)
     sa_copies = [
         remote(stat_s.at[zpeer(d)], stat_r.at[z], sa_s.at[d], sa_r.at[d], zdev(zpeer(d)))
         for d in range(1, nz)
     ]
     stat_r[z] = stat_s[z]
-    back(0, att_full, 0)
     for copy in sa_copies:
         copy.wait_recv()
     features = float(nz * HEAD)
@@ -370,6 +370,7 @@
         remote(stat_f.at[z], stat_f.at[z], sb_s.at[d], sb_r.at[d], zdev(zpeer(d)))
         for d in range(1, nz)
     ]
+    back(0, att_full, 0)
     back(0, att_full, 1)
     for u in range(1, 4):
         sent_in(u)
@@ -401,16 +402,15 @@
         xsend[3, :, o] = nn(gk_t, spots).astype(BF16).T.reshape(npeer, nz, SLOTS, HEAD)
         return 0
 
-    back(0, att_full, 3)
-    lax.fori_loop(0, nz, value_grads, 0)
+    lax.fori_loop(0, nz // 2, value_grads, 0)
+    back(0, att_full, 2)
+    lax.fori_loop(nz // 2, nz, value_grads, 0)
     x_out(1)
-    back(0, att_full, 2)
     lax.fori_loop(0, 4, score_grads, 0)
     for u in range(4):
         block_wait(zbuf.at[u, 1:nz], zin_s.at[u])
     back(1, gv_ref, 3)
     lax.fori_loop(4, 6, score_grads, 0)
-    back(1, gv_ref, 2)
 
     block_wait(att_full, zo_r.at[0])
 
@@ -452,9 +452,9 @@
     pair = remote(
         wbuf.at[0:ny, theirs], pair_recv, pr_s.at[0], pr_r.at[0], pdev(chip * 2 + 1 - core)
     )
+    back(1, gv_ref, 2)
     lax.fori_loop(6, nz, score_grads, 0)
     x_out(2, (3, 2, 1))
-    back(1, gv_ref, 1)
     pair.wait_recv()
 
     def sum_pair(j, _):
@@ -467,8 +467,10 @@
         for d in range(1, ny)
     ]
     dw_recv[y] = wbuf[y, mine]
+    back(1, gv_ref, 1)
     back(1, gv_ref, 0)
     back(2, gq_ref, 3)
+    back(2, gq_ref, 2)
 
     for copy in dy_copies:
         copy.wait_recv()
@@ -492,7 +494,7 @@
         )
     r1_recv[chip] = r1_send[chip]
     x_out(2, (0,))
-    back(2, gq_ref, 2)
+    x_out(3)
     for copy in dp_copies:
         copy.wait_recv()
     acc = r1_recv[0].astype(F32)
@@ -505,7 +507,6 @@
         for d in range(1, nz)
     ]
     r2_recv[z] = r2_send[z]
-    x_out(3, (3, 2))
     back(2, gq_ref, 1)
     back(2, gq_ref, 0)
     for copy in dz_copies:
@@ -517,9 +518,9 @@
     az_copies = [
         remote(gz.at[z], gz.at[z], az_s.at[d], az_r.at[d], zdev(zpeer(d))) for d in range(1, nz)
     ]
-    x_out(3, (1, 0))
     back(3, gk_ref, 3)
     back(3, gk_ref, 2)
+    back(3, gk_ref, 1)
     for copy in az_copies:
         copy.wait_recv()
     place = core * chips + chip
@@ -528,7 +529,6 @@
         remote(gw_ref.at[place], gw_ref.at[place], ap_s.at[d], ap_r.at[d], pdev(ppeer(d)))
         for d in range(1, npeer)
     ]
-    back(3, gk_ref, 1)
     back(3, gk_ref, 0)
     for copy in ap_copies:
         copy.wait_recv()
@@ -549,14 +549,29 @@
 
 
 def settle(*refs):
-    for src, dst in zip(refs[:5], refs[6:11]):
-        dst[...] = src[...]
-    refs[11][...] = refs[5][...].reshape(refs[11].shape).astype(F32)
+    sources, targets, held, sems = refs[:6], refs[6:12], refs[12:18], refs[18]
+    wide = refs[19]
+    loads = [
+        pltpu.make_async_copy(src, buf, sems.at[i])
+        for i, (src, buf) in enumerate(zip(sources, held))
+    ]
+    for copy in loads:
+        copy.start()
+    stores = []
+    for i in range(5):
+        loads[i].wait()
+        stores.append(pltpu.make_async_copy(held[i], targets[i], sems.at[6 + i]))
+        stores[i].start()
+    loads[5].wait()
+    wide[...] = held[5][...].reshape(wide.shape).astype(F32)
+    stores.append(pltpu.make_async_copy(wide, targets[5], sems.at[11]))
+    stores[5].start()
+    for copy in stores:
+        copy.wait()
 
 
 def body(nz, npeer, ny, queries, keys, values, gates, cotangent, hist_len, token_owner, token_row, w_out):
     rows, width = queries.shape
-    lengths = jnp.pad(hist_len, ((0, 0), (0, 120)))
     slots = nz * npeer * SLOTS
     wrows = w_out.shape[0]
     part = wrows // npeer
@@ -621,19 +636,20 @@
         ),
     )(
         queries, keys, values, gates, cotangent,
-        token_owner.reshape(1, rows), token_row.reshape(1, rows), lengths, w_out,
+        token_owner.reshape(1, rows), token_row.reshape(1, rows), hist_len, w_out,
     )
     out, gq, gk, gv, gg, gw = out
-    steps = 4
-    block = pl.BlockSpec((rows // steps, width), lambda i: (i, 0))
-    gq, gk, gv, out, gg, gw = pl.pallas_call(
+    hbm = pl.BlockSpec(memory_space=pltpu.HBM)
+    whole = jax.ShapeDtypeStruct((wrows, width), F32)
+    gk, gq, gv, out, gg, gw = pl.pallas_call(
         settle,
-        grid=(steps,),
-        out_shape=(wide,) * 5 + (jax.ShapeDtypeStruct((wrows, width), F32),),
-        in_specs=[block] * 5 + [pl.BlockSpec((npeer // steps, part, width), lambda i: (i, 0, 0))],
-        out_specs=(block,) * 5 + (pl.BlockSpec((wrows // steps, width), lambda i: (i, 0)),),
+        out_shape=(wide,) * 5 + (whole,),
+        in_specs=[hbm] * 6,
+        out_specs=(hbm,) * 6,
+        scratch_shapes=[pltpu.VMEM((rows, width), BF16)] * 5
+        + [pltpu.VMEM((npeer, part, width), BF16), dma((12,)), pltpu.VMEM((wrows, width), F32)],
         compiler_params=pltpu.CompilerParams(vmem_limit_bytes=60 * 1024 * 1024),
-    )(gq, gk, gv, out, gg, gw)
+    )(gk, gq, gv, out, gg, gw)
     return out, gq, gk, gv, gg, gw
 
 

time: 241 us -> 239 us (level)
  no operation moved by 1% of the time
where the time goes in v3:
time: 239 us
  Pallas kernels  238 us (100%)
    pallas_call x1, Pallas kernels, body(): pl.pallas_call(functools.partial(kernel, nz, npeer, ny), out_shape=(wide,...  233 us
    pallas_call x1, Pallas kernels, body(): pl.pallas_call(settle, out_shape=(wide,) * 5 + (whole,), in_specs=[hbm] *...  4.97 us

profile of v3, /device:TPU:1, one launch (start us, length us, event | category | flops | bytes accessed | tf_op | source)
XLA Modules:
  0.0 238.6 jit_solution(2273694232737860826)
XLA Ops:
  0.6 232.8 %shard_map.136 = (bf16[512,1024]{1,0:T(8,128)(2,1)}, bf16[512,1024]{1,0:T(8,128)(2,1)}, bf16[512,1024]{1,0:T(8,128)(2,1)}, bf16[512,1024]{1,0:T(8,128)(2,1)}, bf...) custom-call(bf16[512,1024]{1,0:T(8,128)(2,1)} %q_ref.1, bf16[512,1024]{1,0:T(8,128)(2,1)} %k_ref.1, ...), custom_call_target="tpu_custom_call" | custom-call | tf_op jit(solution)/shard_map/pallas_call | solution.py:582
  233.4 5.0 %shard_map.137 = (bf16[512,1024]{1,0:T(8,128)(2,1)}, bf16[512,1024]{1,0:T(8,128)(2,1)}, bf16[512,1024]{1,0:T(8,128)(2,1)}, bf16[512,1024]{1,0:T(8,128)(2,1)}, bf...) custom-call(bf16[512,1024]{1,0:T(8,128)(2,1)} %get-tuple-element.18.refs_0_, bf16[512,1024]{1,0:T(8,128)(2,1)} %get-tuple-element.19.refs_1_, ...), custom_call_target="tpu_custom_call" | custom-call | tf_op jit(solution)/shard_map/pallas_call | solution.py:644

commit v4 on v3

--- a/solution.py
+++ b/solution.py
@@ -284,9 +284,9 @@
     pack_in(3, 1)
     pack_in(3, 2)
     unpack_in(2)
-    pack_in(3, 3)
     sent_in(0)
     lax.fori_loop(0, nz // 2, attend, 0)
+    pack_in(3, 3)
     pack_in(3, 4)
     lax.fori_loop(nz // 2, nz, attend, 0)
 
@@ -325,7 +325,7 @@
                     zdev(zpeer(nz - order[j])),
                 )
 
-    x_out(0, (3, 0, 1, 2))
+    x_out(0, (0, 1, 3, 2))
 
     block_wait(xrecv.at[3], xin_r.at[3])
 
@@ -346,9 +346,7 @@
         stat_s[o] = table.T[0:8, :]
         return 0
 
-    lax.fori_loop(0, nz // 2, stats, 0)
-    back(0, att_full, 3)
-    lax.fori_loop(nz // 2, nz, stats, 0)
+    lax.fori_loop(0, nz, stats, 0)
     sa_copies = [
         remote(stat_s.at[zpeer(d)], stat_r.at[z], sa_s.at[d], sa_r.at[d], zdev(zpeer(d)))
         for d in range(1, nz)
@@ -371,7 +369,6 @@
         for d in range(1, nz)
     ]
     back(0, att_full, 0)
-    back(0, att_full, 1)
     for u in range(1, 4):
         sent_in(u)
     for copy in sb_copies:
@@ -402,15 +399,20 @@
         xsend[3, :, o] = nn(gk_t, spots).astype(BF16).T.reshape(npeer, nz, SLOTS, HEAD)
         return 0
 
+    back(0, att_full, 1)
     lax.fori_loop(0, nz // 2, value_grads, 0)
-    back(0, att_full, 2)
+    back(0, att_full, 3)
     lax.fori_loop(nz // 2, nz, value_grads, 0)
     x_out(1)
+    back(0, att_full, 2)
     lax.fori_loop(0, 4, score_grads, 0)
     for u in range(4):
         block_wait(zbuf.at[u, 1:nz], zin_s.at[u])
     back(1, gv_ref, 3)
-    lax.fori_loop(4, 6, score_grads, 0)
+    lax.fori_loop(4, nz, score_grads, 0)
+    x_out(2)
+    back(1, gv_ref, 2)
+    back(1, gv_ref, 1)
 
     block_wait(att_full, zo_r.at[0])
 
@@ -452,9 +454,7 @@
     pair = remote(
         wbuf.at[0:ny, theirs], pair_recv, pr_s.at[0], pr_r.at[0], pdev(chip * 2 + 1 - core)
     )
-    back(1, gv_ref, 2)
-    lax.fori_loop(6, nz, score_grads, 0)
-    x_out(2, (3, 2, 1))
+    back(1, gv_ref, 0)
     pair.wait_recv()
 
     def sum_pair(j, _):
@@ -467,10 +467,9 @@
         for d in range(1, ny)
     ]
     dw_recv[y] = wbuf[y, mine]
-    back(1, gv_ref, 1)
-    back(1, gv_ref, 0)
     back(2, gq_ref, 3)
     back(2, gq_ref, 2)
+    back(2, gq_ref, 1)
 
     for copy in dy_copies:
         copy.wait_recv()
@@ -493,8 +492,8 @@
             )
         )
     r1_recv[chip] = r1_send[chip]
-    x_out(2, (0,))
     x_out(3)
+    back(2, gq_ref, 0)
     for copy in dp_copies:
         copy.wait_recv()
     acc = r1_recv[0].astype(F32)
@@ -507,8 +506,7 @@
         for d in range(1, nz)
     ]
     r2_recv[z] = r2_send[z]
-    back(2, gq_ref, 1)
-    back(2, gq_ref, 0)
+    back(3, gk_ref, 3)
     for copy in dz_copies:
         copy.wait_recv()
     acc = r2_recv[0].astype(F32)
@@ -518,9 +516,9 @@
     az_copies = [
         remote(gz.at[z], gz.at[z], az_s.at[d], az_r.at[d], zdev(zpeer(d))) for d in range(1, nz)
     ]
-    back(3, gk_ref, 3)
     back(3, gk_ref, 2)
     back(3, gk_ref, 1)
+    back(3, gk_ref, 0)
     for copy in az_copies:
         copy.wait_recv()
     place = core * chips + chip
@@ -529,7 +527,6 @@
         remote(gw_ref.at[place], gw_ref.at[place], ap_s.at[d], ap_r.at[d], pdev(ppeer(d)))
         for d in range(1, npeer)
     ]
-    back(3, gk_ref, 0)
     for copy in ap_copies:
         copy.wait_recv()
 

time: 239 us -> 240 us (level); the launches traced: 239 us -> 236 us
  Pallas kernels: 238 us -> 235 us
where the time goes in v4:
time: 240 us; the launch traced here: 236 us
  Pallas kernels  235 us (98%)
    pallas_call x1, Pallas kernels, body(): pl.pallas_call(functools.partial(kernel, nz, npeer, ny), out_shape=(wide,...  230 us
    pallas_call x1, Pallas kernels, body(): pl.pallas_call(settle, out_shape=(wide,) * 5 + (whole,), in_specs=[hbm] *...  4.97 us

profile of v4, /device:TPU:1, one launch (start us, length us, event | category | flops | bytes accessed | tf_op | source)
XLA Modules:
  0.0 236.2 jit_solution(239564905234651426)
XLA Ops:
  0.6 230.5 %shard_map.136 = (bf16[512,1024]{1,0:T(8,128)(2,1)}, bf16[512,1024]{1,0:T(8,128)(2,1)}, bf16[512,1024]{1,0:T(8,128)(2,1)}, bf16[512,1024]{1,0:T(8,128)(2,1)}, bf...) custom-call(bf16[512,1024]{1,0:T(8,128)(2,1)} %q_ref.1, bf16[512,1024]{1,0:T(8,128)(2,1)} %k_ref.1, ...), custom_call_target="tpu_custom_call" | custom-call | tf_op jit(solution)/shard_map/pallas_call | solution.py:579
  231.1 5.0 %shard_map.137 = (bf16[512,1024]{1,0:T(8,128)(2,1)}, bf16[512,1024]{1,0:T(8,128)(2,1)}, bf16[512,1024]{1,0:T(8,128)(2,1)}, bf16[512,1024]{1,0:T(8,128)(2,1)}, bf...) custom-call(bf16[512,1024]{1,0:T(8,128)(2,1)} %get-tuple-element.18.refs_0_, bf16[512,1024]{1,0:T(8,128)(2,1)} %get-tuple-element.19.refs_1_, ...), custom_call_target="tpu_custom_call" | custom-call | tf_op jit(solution)/shard_map/pallas_call | solution.py:641
